TPU v7x, 32 devices: a whole 2x2x4 slice. The times are simulated.
32 devices in a mesh: seq: 8 (over z, core), tensor: 4 (over y, x).
Axes of the slice: x: 2, y: 2, z: 4, core: 2. Of those that a mesh axis runs over, the one named last changes fastest.
Arguments:
- tokens: bfloat16 [2, 1024, 3072], P(None, 'seq'), as said below
- w_query: bfloat16 [3072, 3072], P(None, 'tensor'), as said below
- w_key: bfloat16 [3072, 3072], P(None, 'tensor'), as said below
- w_value: bfloat16 [3072, 3072], P(None, 'tensor'), as said below
- w_out: bfloat16 [3072, 3072], P('tensor'), as said below
- cotangent: bfloat16 [2, 1024, 3072], P(None, 'seq'), may hold values from -6 to 6
- noise_value: float32 [3072, 3072], P('seq', 'tensor'), may hold values from -6 to 6
- noise_out: float32 [3072, 3072], P('tensor', 'seq'), may hold values from -6 to 6
Outputs:
- grad_value: float32 [3072, 3072], P('seq', 'tensor')
- grad_out: float32 [3072, 3072], P('tensor', 'seq')
Inputs may be any that keep to these rules, and one draw needn't show every extreme that they name: `tokens`: patch activations. `w_query`: scaled by the fan-in. `w_key`: scaled by the fan-in. `w_value`: scaled by the fan-in. `w_out`: scaled by the fan-in.
All inputs are finite; a program needn't handle non-finite values.
Results may differ from a plain program's by a relative error of at most 0.023.
Values may be sent and summed in bfloat16 or wider, within the bound.
A program may use at most 128 MiB of HBM per device.

v0:
```python
import math

import jax
import jax.numpy as jnp
from jax import lax
from jax.sharding import PartitionSpec as P

D = 3072
HEADS = 24
HEAD_DIM = 128


def local(tokens, w_query, w_key, w_value, w_out, cotangent, noise_value, noise_out):
    images, patch_rows, width = tokens.shape
    columns = w_query.shape[1]
    head_count = columns // HEAD_DIM
    score_scale = 1.0 / math.sqrt(HEAD_DIM)
    clip_bound = math.sqrt(2.0 * D * HEADS * HEAD_DIM)
    flat_tokens = tokens.reshape(images * patch_rows, width)

    def project(weight):
        product = jnp.dot(flat_tokens, weight, preferred_element_type=jnp.float32)
        return product.astype(jnp.bfloat16).reshape(images, patch_rows, head_count, HEAD_DIM)

    queries = project(w_query)
    key_local = project(w_key)
    value_local = project(w_value)
    keys_all, values_all = (
        lax.all_gather(key_local, "seq", axis=1, tiled=True),
        lax.all_gather(value_local, "seq", axis=1, tiled=True),
    )
    scores = (
        jnp.einsum("iqhd,ikhd->ihqk", queries, keys_all, preferred_element_type=jnp.float32)
        * score_scale
    )
    row_totals = jax.nn.logsumexp(scores, axis=-1)
    attn_probs = jnp.exp(scores - row_totals[..., None]).astype(jnp.bfloat16)
    attended = jnp.einsum(
        "ihqk,ikhd->iqhd", attn_probs, values_all, preferred_element_type=jnp.float32
    ).astype(jnp.bfloat16)
    flat_cotangent = cotangent.reshape(images * patch_rows, width)
    d_attn = jnp.einsum("rd,cd->rc", flat_cotangent, w_out, preferred_element_type=jnp.float32)
    d_attn = d_attn.astype(jnp.bfloat16).reshape(images, patch_rows, head_count, HEAD_DIM)
    summed = lax.psum_scatter(
        jnp.einsum(
            "ihqk,iqhd->kihd", attn_probs, d_attn, preferred_element_type=jnp.float32
        ).astype(jnp.bfloat16),
        "seq",
        scatter_dimension=0,
        tiled=True,
    )
    product = jnp.einsum("iqhd,iqe->ihde", attended, cotangent, preferred_element_type=jnp.float32)
    value_product = jnp.einsum("ipe,pihd->iehd", tokens, summed, preferred_element_type=jnp.float32)
    value_shard = lax.psum_scatter(
        value_product.reshape(images, width, columns).astype(jnp.bfloat16),
        "seq",
        scatter_dimension=1,
        tiled=True,
    ).astype(jnp.float32)
    out_shard = lax.psum_scatter(
        product.reshape(images, columns, width).astype(jnp.bfloat16),
        "seq",
        scatter_dimension=2,
        tiled=True,
    ).astype(jnp.float32)
    partial_value = jnp.sum(jnp.square(value_shard), axis=(1, 2)) + jnp.sum(
        jnp.square(out_shard), axis=(1, 2)
    )
    squares_all = lax.psum(partial_value, ("seq", "tensor"))
    factor = clip_bound / (jnp.sqrt(squares_all) + 0.01)
    grad_value = noise_value
    grad_out = noise_out
    for image_index in range(images):
        grad_value = grad_value + factor[image_index] * value_shard[image_index]
        grad_out = grad_out + factor[image_index] * out_shard[image_index]
    return (grad_value / images, grad_out / images)


def solution(mesh):
    placed = (
        P(None, "seq", None),
        P(None, "tensor"),
        P(None, "tensor"),
        P(None, "tensor"),
        P("tensor", None),
        P(None, "seq", None),
        P("seq", "tensor"),
        P("tensor", "seq"),
    )
    return jax.shard_map(
        local,
        mesh=mesh,
        in_specs=placed,
        out_specs=(P("seq", "tensor"), P("tensor", "seq")),
        check_vma=False,
    )
```

profile of v0, /device:TPU:0, one launch (start us, length us, event | category | flops | bytes accessed | tf_op | source)
XLA Modules:
  0.0 392.7 jit_solution(17421297260059780231)
XLA Ops:
  7.2 1.4 copy-done
  8.6 3.7 convolution_convert_fusion.5
  12.8 0.8 copy.23
  13.6 3.7 convolution_convert_fusion.4
  17.8 1.0 copy.28
  18.9 3.7 convolution_convert_fusion.6
  22.7 0.5 reshape.54
  23.1 4.6 %convolution_convert_fusion.7 = bf16[256,768]{1,0:T(8,128)(2,1)S(1)} fusion(bf16[256,3072]{1,0:T(8,128)(2,1)} %bitcast.76, bf16[768,3072]{1,0:T(8,128)(2,1)} %param.12), kind=kOutput, calls=%fused_computation.14 | convolution fusion | flops 1208156160 | bytes 6684672 | tf_op jit(solution)/shard_map/rd,cd->rc/dot_general | solution.py:42
  27.7 0.5 reshape.53
  28.2 26.5 %all-gather.3.cloned.1.call-done = bf16[2,1024,6,128]{3,1,2,0:T(8,128)(2,1)} async-done(((bf16[2,128,6,128]{3,1,2,0:T(8,128)(2,1)}), bf16[2,1024,6,128]{3,1,2,0:T(8,128)(2,1)}) %all-gather.3.cloned.1.call-update) | async-done | bytes 3145744 | tf_op jit(solution)/shard_map/all_gather | solution.py:29
  54.7 2.9 multiply_reduce_fusion
  57.7 1.3 exponential_reduce_fusion
  59.0 1.3 copy-done.1
  60.4 3.2 convolution_convert_fusion.2
  63.6 4.7 %copy.43 = bf16[1024,1536]{1,0:T(8,128)(2,1)} copy(bf16[1024,1536]{0,1:T(8,128)(2,1)} %bitcast.73) | data formatting | bytes 6291456
  68.6 26.4 %all-gather.5.cloned.1.call-done = bf16[2,1024,6,128]{1,3,2,0:T(8,128)(2,1)} async-done(((bf16[2,128,6,128]{1,3,2,0:T(8,128)(2,1)}), bf16[2,1024,6,128]{1,3,2,0:T(8,128)(2,1)}) %all-gather.5.cloned.1.call-update) | async-done | bytes 3145744 | tf_op jit(solution)/shard_map/all_gather | solution.py:30
  95.0 11.5 %convolution_convert_fusion = bf16[2,6,128,3072]{3,2,1,0:T(8,128)(2,1)} fusion(bf16[2,128,3072]{2,1,0:T(8,128)(2,1)S(1)} %copy-done.3, bf16[2,1024,6,128]{1,3,2,0:T(8,128)(2,1)} %all-gather.5.cloned.1.call-done, f32[2,6,128,1024]{3,2,1,0:T(8,128)} %copy-done.1, f32[2,6,128]{2,1,0:T(8,128)S(1)} %log_add_fusion), kind=kOutput, calls=%fused_computation | convolution fusion | flops 1620246528 | bytes 20453376 | tf_op jit(solution)/shard_map/iqhd,iqe->ihde/dot_general | solution.py:52
  106.5 24.0 %copy.41 = bf16[2,768,3072]{1,0,2:T(2,128)(2,1)} copy(bf16[2,768,3072]{2,1,0:T(8,128)(2,1)} %bitcast.70) | data formatting | bytes 18874368
  130.4 9.0 %copy.45 = bf16[384,8,2,768]{3,1,2,0:T(8,128)(2,1)} copy(bf16[384,8,2,768]{3,2,1,0:T(2,128)(2,1)} %bitcast.71) | data formatting | bytes 18874368
  139.5 1.2 copy.44
  140.8 5.3 %convolution_convert_fusion.1 = bf16[2,6,128,3072]{3,2,1,0:T(8,128)(2,1)} fusion(bf16[128,2,6,128]{0,3,2,1:T(8,128)(2,1)S(1)} %bitcast.75, bf16[2,128,3072]{2,1,0:T(8,128)(2,1)S(1)} %copy-done), kind=kOutput, calls=%fused_computation.1 | convolution fusion | flops 1212678144 | bytes 11403264 | tf_op jit(solution)/shard_map/ipe,pihd->iehd/dot_general | solution.py:53
  146.0 12.7 %copy.26 = bf16[2,3072,768]{2,1,0:T(8,128)(2,1)} copy(bf16[2,3072,768]{1,2,0:T(8,128)(2,1)} %bitcast.72) | data formatting | bytes 18874368 | tf_op jit(solution)/shard_map/convert_element_type | solution.py:55
  158.8 78.6 %reduce-scatter.12.cloned.1.call-done = bf16[384,1536]{1,0:T(8,128)(2,1)} async-done(((bf16[3072,1536]{1,0:T(8,128)(2,1)}), bf16[384,1536]{1,0:T(8,128)(2,1)}) %reduce-scatter.12.cloned.1.call-update) | async-done | bytes 1179664
  237.4 3.7 reshape.60
  241.1 3.7 copy.42
  245.2 92.3 %reduce-scatter.8.cloned.1.call-done = bf16[2,384,768]{2,1,0:T(8,128)(2,1)} async-done(((bf16[2,3072,768]{2,1,0:T(8,128)(2,1)}), bf16[2,384,768]{2,1,0:T(8,128)(2,1)}) %reduce-scatter.8.cloned.1.call-update) | async-done | bytes 1179664 | tf_op jit(solution)/shard_map/reduce_scatter | solution.py:54
  337.5 1.7 multiply_reduce_fusion.2
  339.2 1.6 convert_element_type.63
  340.7 37.7 %psum.7 = f32[2]{0:T(128)S(1)} all-reduce(f32[2]{0:T(128)S(1)} %add.34), channel_id=1, replica_groups=mesh['seq'=8,'tensor'=4] {'seq','tensor'}, use_global_device_ids=true, to_apply=%region_7.0 | all-reduce | flops 2 | bytes 16 | tf_op jit(solution)/shard_map/psum | solution.py:69
  378.5 0.6 fusion.19
  379.1 4.5 %fusion.5 = f32[768,384]{1,0:T(8,128)} fusion(f32[2,768,384]{2,1,0:T(8,128)} %convert_element_type.63, f32[768,384]{1,0:T(8,128)} %param.15, f32[]{:T(128)} %bitcast.13, f32[]{:T(128)} %bitcast.11), kind=kLoop, calls=%fused_computation.19 | loop fusion | flops 1474560 | bytes 4718600 | tf_op jit(solution)/shard_map/div | solution.py:76
  383.8 2.4 fusion.10
  (27 shorter events, 2.0 us)
Async XLA Ops:
  7.2 1.4 copy-start
  7.2 47.6 %all-gather.3.cloned.1.call-start = ((), (), s32[]{:S(2)}) async-start(), calls=%async_computation.3 | async-start | bytes 3538944 | tf_op jit(solution)/shard_map/all_gather | solution.py:29
  13.6 81.4 %all-gather.5.cloned.1.call-start = ((), (), s32[]{:S(2)}) async-start(), calls=%async_computation.5 | async-start | bytes 3538944 | tf_op jit(solution)/shard_map/all_gather | solution.py:30
  18.9 120.6 %reduce-scatter.10.cloned.1.call-start = ((), (), s32[]{:S(2)}) async-start(), calls=%async_computation.6 | async-start | bytes 3538944
  57.7 2.7 copy-start.1
  68.3 26.6 %copy-start.3 = (bf16[2,128,3072]{2,1,0:T(8,128)(2,1)S(1)}, bf16[2,128,3072]{2,1,0:T(8,128)(2,1)}, u32[]{:S(2)}) copy-start(bf16[2,128,3072]{2,1,0:T(8,128)(2,1)} %param.13) | copy-start | bytes 4718596
  68.4 169.0 %reduce-scatter.12.cloned.1.call-start = ((), (), s32[]{:S(2)}) async-start(), calls=%async_computation.7 | async-start | bytes 10616832
  139.5 198.0 %reduce-scatter.8.cloned.1.call-start = ((), (), s32[]{:S(2)}) async-start(), calls=%async_computation.4 | async-start | bytes 10616832 | tf_op jit(solution)/shard_map/reduce_scatter | solution.py:54
  340.7 42.8 %copy-start.2 = (bf16[2,384,768]{2,1,0:T(8,128)(2,1)S(1)}, bf16[2,384,768]{2,1,0:T(8,128)(2,1)}, u32[]{:S(2)}) copy-start(bf16[2,384,768]{2,1,0:T(8,128)(2,1)} %reduce-scatter.8.cloned.1.call-done) | copy-start | bytes 3538948
  379.1 4.7 %copy-start.4 = (f32[384,768]{1,0:T(8,128)S(1)}, f32[384,768]{1,0:T(8,128)}, u32[]{:S(2)}) copy-start(f32[384,768]{1,0:T(8,128)} %param.14) | copy-start | bytes 3538948
Sparse Core Ops, SparseCore 0:
  13.7 40.9 all-gather.2
  56.9 38.0 all-gather.4
  97.3 38.5 reduce-scatter.9
  139.6 97.7 reduce-scatter.11
  239.6 97.8 reduce-scatter.7
where the time goes:
time: 395 us; the launch traced here: 393 us
  waiting for transfers between devices  224 us (57%)
  local copies, waits for them, and re-layouts  66 us (17%)
  matrix products  38.7 us (10%)
  blocking collectives  37.7 us (10%)
  between operations  13.9 us (4%)
  other arithmetic  12.1 us (3%)
    reduce_scatter x1, waiting for transfers between devices, local(): lax.psum_scatter(value_product.reshape(images, width, columns).astype(jnp...  92.3 us
    unnamed x7, waiting for transfers between devices  78.7 us
    unnamed x16, local copies, waits for them, and re-layouts  49 us
    psum x1, blocking collectives, local(): squares_all = lax.psum(partial_value, ('seq', 'tensor'))  37.7 us
    all_gather x1, waiting for transfers between devices, local(): lax.all_gather(key_local, 'seq', axis=1, tiled=True)  26.5 us
    all_gather x1, waiting for transfers between devices, local(): lax.all_gather(value_local, 'seq', axis=1, tiled=True)  26.4 us
    convert_element_type x1, local copies, waits for them, and re-layouts, local(): value_product.reshape(images, width, columns).astype(jnp.bfloat16)  12.7 us
    dot_general x1, matrix products, local(): jnp.einsum('iqhd,iqe->ihde', attended, cotangent, preferred_element_type=...  11.5 us
  transfers between devices with their start and end apart: 5, of which 4 were waited for; matrix products, arithmetic and copies ran while one was open for 25% of the time, Pallas kernels for 0%

commit v1 on v0

v1 whole, which is shorter than its diff:
```python
import math

import jax
import jax.numpy as jnp
from jax import lax
from jax.sharding import PartitionSpec as P

HEAD_DIM = 128


def local(tokens, w_query, w_key, w_value, w_out, cotangent, noise_value, noise_out):
    images, patch_rows, width = tokens.shape
    columns = w_query.shape[1]
    head_count = columns // HEAD_DIM
    score_scale = 1.0 / math.sqrt(HEAD_DIM)
    clip_bound = math.sqrt(2.0 * width * width)
    flat_tokens = tokens.reshape(images * patch_rows, width)

    token_columns = lax.all_to_all(tokens, "seq", split_axis=2, concat_axis=1, tiled=True)
    cot_columns = lax.all_to_all(cotangent, "seq", split_axis=2, concat_axis=1, tiled=True)

    def heads_first(rows):
        split = rows.reshape(images, patch_rows, head_count, HEAD_DIM)
        return split.transpose(0, 2, 1, 3)

    def project(weight):
        product = jnp.dot(flat_tokens, weight, preferred_element_type=jnp.float32)
        return product.astype(jnp.bfloat16)

    key_local = heads_first(project(w_key))
    keys_all = lax.all_gather(key_local, "seq", axis=2, tiled=True)
    value_local = heads_first(project(w_value))
    values_all = lax.all_gather(value_local, "seq", axis=2, tiled=True)
    queries = heads_first(project(w_query))
    flat_cotangent = cotangent.reshape(images * patch_rows, width)
    d_attn = jnp.einsum("rd,cd->rc", flat_cotangent, w_out, preferred_element_type=jnp.float32)
    d_attn = heads_first(d_attn.astype(jnp.bfloat16))
    scores = (
        jnp.einsum("ihqd,ihkd->ihqk", queries, keys_all, preferred_element_type=jnp.float32)
        * score_scale
    )
    row_totals = jax.nn.logsumexp(scores, axis=-1)
    attn_probs = jnp.exp(scores - row_totals[..., None]).astype(jnp.bfloat16)
    d_value = jnp.einsum(
        "ihqk,ihqd->ihkd", attn_probs, d_attn, preferred_element_type=jnp.float32
    ).astype(jnp.bfloat16)
    d_value = lax.psum_scatter(d_value, "seq", scatter_dimension=2, tiled=True)
    d_value_all = lax.all_gather(d_value, "seq", axis=2, tiled=True)
    attended = jnp.einsum(
        "ihqk,ihkd->ihqd", attn_probs, values_all, preferred_element_type=jnp.float32
    ).astype(jnp.bfloat16)
    attended_all = lax.all_gather(attended, "seq", axis=2, tiled=True)

    per_value = jnp.einsum(
        "ipe,ihpd->iehd", token_columns, d_value_all, preferred_element_type=jnp.float32
    ).reshape(images, -1, columns)
    per_out = jnp.einsum(
        "ihpd,ipe->ihde", attended_all, cot_columns, preferred_element_type=jnp.float32
    ).reshape(images, columns, -1)
    partial = jnp.sum(jnp.square(per_value), axis=(1, 2)) + jnp.sum(jnp.square(per_out), axis=(1, 2))
    squares = lax.psum(partial, ("seq", "tensor"))
    factor = clip_bound / (jnp.sqrt(squares) + 0.01)
    grad_value = noise_value
    grad_out = noise_out
    for image_index in range(images):
        grad_value = grad_value + factor[image_index] * per_value[image_index]
        grad_out = grad_out + factor[image_index] * per_out[image_index]
    return (grad_value / images, grad_out / images)


def solution(mesh):
    placed = (
        P(None, "seq", None),
        P(None, "tensor"),
        P(None, "tensor"),
        P(None, "tensor"),
        P("tensor", None),
        P(None, "seq", None),
        P("seq", "tensor"),
        P("tensor", "seq"),
    )
    return jax.shard_map(
        local,
        mesh=mesh,
        in_specs=placed,
        out_specs=(P("seq", "tensor"), P("tensor", "seq")),
        check_vma=False,
    )
```

time: 395 us -> 339 us (0.86)
  waiting for transfers between devices: 224 us -> 187 us
  local copies, waits for them, and re-layouts: 66 us -> 36 us
  starting transfers between devices: 0.39 us -> 16.7 us
    reduce_scatter x1 -> x0, waiting for transfers between devices: 92.3 us -> none  [local(): lax.psum_scatter(value_product.reshape(images, width, columns).astype(jnp...]
    all_to_all x0 -> x2, waiting for transfers between devices: none -> 58.3 us  [the longest x1 58.3 us: local(): lax.all_to_all(tokens, 'seq', split_axis=2, concat_axis=1, tiled=True)]
    unnamed x7 -> x6, waiting for transfers between devices: 78.7 us -> 52.3 us
    unnamed x16 -> x22, local copies, waits for them, and re-layouts: 49 us -> 23.5 us
    all_gather x2 -> x4, waiting for transfers between devices: 52.9 us -> 76 us  [the longest x1 28.8 us: local(): d_value_all = lax.all_gather(d_value, 'seq', axis=2, tiled=True)]
    all_to_all x0 -> x2, starting transfers between devices: none -> 16.1 us  [the longest x1 12.5 us: local(): lax.all_to_all(tokens, 'seq', split_axis=2, concat_axis=1, tiled=True)]
    convert_element_type x1 -> x2, local copies, waits for them, and re-layouts: 12.7 us -> 0.34 us  [the longest x1 0.17 us: project(): return product.astype(jnp.bfloat16)]
    all_to_all x0 -> x2, local copies, waits for them, and re-layouts: none -> 6.03 us  [the longest x1 3.03 us: local(): lax.all_to_all(tokens, 'seq', split_axis=2, concat_axis=1, tiled=True)]
  transfers between devices with their start and end apart: 5 -> 7, of which waited for: 4 -> 5; matrix products, arithmetic and copies ran while one was open for 25% -> 17% of each run, Pallas kernels for 0% -> 0%
where the time goes in v1:
time: 339 us; the launch traced here: 338 us
  waiting for transfers between devices  187 us (55%)
  blocking collectives  38.5 us (11%)
  matrix products  36.9 us (11%)
  local copies, waits for them, and re-layouts  36 us (11%)
  starting transfers between devices  16.7 us (5%)
  between operations  13.9 us (4%)
  other arithmetic  9.29 us (3%)
    all_to_all x1, waiting for transfers between devices, local(): lax.all_to_all(tokens, 'seq', split_axis=2, concat_axis=1, tiled=True)  58.3 us
    unnamed x6, waiting for transfers between devices  52.3 us
    psum x1, blocking collectives, local(): squares = lax.psum(partial, ('seq', 'tensor'))  38.5 us
    all_gather x1, waiting for transfers between devices, local(): d_value_all = lax.all_gather(d_value, 'seq', axis=2, tiled=True)  28.8 us
    all_gather x1, waiting for transfers between devices, local(): keys_all = lax.all_gather(key_local, 'seq', axis=2, tiled=True)  27.3 us
    unnamed x22, local copies, waits for them, and re-layouts  23.5 us
    all_gather x1, waiting for transfers between devices, local(): values_all = lax.all_gather(value_local, 'seq', axis=2, tiled=True)  20 us
    all_to_all x1, starting transfers between devices, local(): lax.all_to_all(tokens, 'seq', split_axis=2, concat_axis=1, tiled=True)  12.5 us
  transfers between devices with their start and end apart: 7, of which 5 were waited for; matrix products, arithmetic and copies ran while one was open for 17% of the time, Pallas kernels for 0%

profile of v1, /device:TPU:0, one launch (start us, length us, event | category | flops | bytes accessed | tf_op | source)
XLA Modules:
  0.0 338.0 jit_solution(3576360967054562471)
XLA Ops:
  7.2 4.3 %convolution_convert_fusion.4 = bf16[256,768]{1,0:T(8,128)(2,1)S(1)} fusion(bf16[256,3072]{1,0:T(8,128)(2,1)} %bitcast.72, bf16[3072,768]{1,0:T(8,128)(2,1)} %param.10), kind=kOutput, calls=%fused_computation.11 | convolution fusion | flops 1208156160 | bytes 6684672 | tf_op jit(solution)/shard_map/dot_general | solution.py:27
  12.9 3.7 %convolution_convert_fusion.2 = bf16[256,768]{1,0:T(8,128)(2,1)S(1)} fusion(bf16[256,3072]{1,0:T(8,128)(2,1)S(1)} %bitcast.73, bf16[3072,768]{1,0:T(8,128)(2,1)} %param.11), kind=kOutput, calls=%fused_computation.9 | convolution fusion | flops 1208156160 | bytes 6684672 | tf_op jit(solution)/shard_map/dot_general | solution.py:27
  18.1 3.8 %convolution_convert_fusion.5 = bf16[256,768]{1,0:T(8,128)(2,1)S(1)} fusion(bf16[256,3072]{1,0:T(8,128)(2,1)S(1)} %bitcast.74, bf16[3072,768]{1,0:T(8,128)(2,1)} %param.9), kind=kOutput, calls=%fused_computation.12 | convolution fusion | flops 1208156160 | bytes 6684672 | tf_op jit(solution)/shard_map/dot_general | solution.py:27
  22.3 4.1 %convolution_convert_fusion.3 = bf16[256,768]{1,0:T(8,128)(2,1)S(1)} fusion(bf16[256,3072]{1,0:T(8,128)(2,1)S(1)} %bitcast.71, bf16[768,3072]{1,0:T(8,128)(2,1)} %param.12), kind=kOutput, calls=%fused_computation.10 | convolution fusion | flops 1208156160 | bytes 6684672 | tf_op jit(solution)/shard_map/rd,cd->rc/dot_general | solution.py:36
  26.7 27.3 %all-gather.5.cloned.1.call-done = bf16[2,6,1024,128]{3,2,1,0:T(8,128)(2,1)} async-done(((bf16[2,6,128,128]{3,2,1,0:T(8,128)(2,1)}), bf16[2,6,1024,128]{3,2,1,0:T(8,128)(2,1)}) %all-gather.5.cloned.1.call-update) | async-done | bytes 3145744 | tf_op jit(solution)/shard_map/all_gather | solution.py:31
  54.0 3.0 multiply_reduce_fusion
  57.0 1.3 exponential_reduce_fusion
  58.3 1.4 copy-done
  59.6 1.9 convolution_convert_fusion
  61.5 4.2 %copy.63 = bf16[2,6,1024,128]{3,1,0,2:T(8,128)(2,1)} copy(bf16[2,6,1024,128]{3,2,1,0:T(8,128)(2,1)S(1)} %convolution_convert_fusion) | data formatting | bytes 6291456
  65.7 7.6 %reshape.61 = bf16[1024,1536]{1,0:T(8,128)(2,1)} reshape(bf16[1024,2,6,128]{3,2,1,0:T(8,128)(2,1)} %bitcast.63) | data formatting | bytes 6291456
  73.4 20.0 %all-gather.9.cloned.1.call-done = bf16[2,6,1024,128]{3,2,1,0:T(8,128)(2,1)} async-done(((bf16[2,6,128,128]{3,2,1,0:T(8,128)(2,1)}), bf16[2,6,1024,128]{3,2,1,0:T(8,128)(2,1)}) %all-gather.9.cloned.1.call-update) | async-done | bytes 3145744 | tf_op jit(solution)/shard_map/all_gather | solution.py:33
  93.3 5.8 %convolution_convert_fusion.1 = bf16[2,6,128,128]{3,2,1,0:T(8,128)(2,1)} fusion(bf16[2,6,1024,128]{3,2,1,0:T(8,128)(2,1)} %all-gather.9.cloned.1.call-done, f32[2,6,128,1024]{3,2,1,0:T(8,128)} %copy-done, f32[2,6,128]{2,1,0:T(8,128)S(1)} %log_add_fusion), kind=kOutput, calls=%fused_computation.8 | convolution fusion | flops 407568384 | bytes 9836544 | tf_op jit(solution)/shard_map/ihqk,ihkd->ihqd/dot_general | solution.py:49
  99.2 2.9 copy.38
  102.1 3.6 %all-to-all-start.1 = ((bf16[2,128,3072]{1,0,2:T(2,128)(2,1)}), bf16[2,128,3072]{1,0,2:T(2,128)(2,1)S(1)}, u32[]{:S(2)}, u32[]{:S(2)}) async-start(bf16[2,128,3072]{1,0,2:T(2,128)(2,1)} %copy.38), calls=%async_computation.1 | async-start | bytes 3145728 | tf_op jit(solution)/shard_map/all_to_all | solution.py:20
  105.9 52.3 %reduce-scatter.4.cloned.1.call-done = bf16[128,1536]{1,0:T(8,128)(2,1)} async-done(((bf16[1024,1536]{1,0:T(8,128)(2,1)}), bf16[128,1536]{1,0:T(8,128)(2,1)}) %reduce-scatter.4.cloned.1.call-update) | async-done | bytes 393232
  158.2 1.4 reshape.62
  160.8 4.9 %copy.34 = bf16[2,128,3072]{1,0,2:T(2,128)(2,1)} copy(bf16[2,128,3072]{2,1,0:T(8,128)(2,1)} %param.8) | data formatting | bytes 3145728 | tf_op args[0]
  165.7 12.5 %all-to-all-start = ((bf16[2,128,3072]{1,0,2:T(2,128)(2,1)}), bf16[2,128,3072]{1,0,2:T(2,128)(2,1)S(1)}, u32[]{:S(2)}, u32[]{:S(2)}) async-start(bf16[2,128,3072]{1,0,2:T(2,128)(2,1)} %copy.34), calls=%async_computation | async-start | bytes 3145728 | tf_op jit(solution)/shard_map/all_to_all | solution.py:19
  178.2 3.0 copy.39
  181.2 58.3 %all-to-all-done = bf16[2,128,3072]{1,0,2:T(2,128)(2,1)S(1)} async-done(((bf16[2,128,3072]{1,0,2:T(2,128)(2,1)}), bf16[2,128,3072]{1,0,2:T(2,128)(2,1)S(1)}, u32[]{:S(2)}, u32[]{:S(2)}) %all-to-all-start) | async-done | bytes 1572896 | tf_op jit(solution)/shard_map/all_to_all | solution.py:19
  239.5 3.0 copy.35
  242.5 4.6 %multiply_reduce_fusion.1 = (f32[2]{0:T(128)S(1)}, f32[2,6,128,384]{3,2,1,0:T(8,128)S(1)}) fusion(bf16[2,6,1024,128]{3,2,1,0:T(8,128)(2,1)} %all-gather.11.cloned.1.call-done, bf16[2,1024,384,1]{2,1,3,0:T(8,128)(2,1)} %bitcast.76), kind=kOutput, calls=%fused_computation.4 | convolution fusion | flops 1209139200 | bytes 7077896 | tf_op jit(solution)/shard_map/ihpd,ipe->ihde/dot_general | solution.py:57
  247.1 28.8 %all-gather.7.cloned.1.call-done = bf16[2,6,1024,128]{2,3,1,0:T(8,128)(2,1)} async-done(((bf16[2,6,128,128]{2,3,1,0:T(8,128)(2,1)}), bf16[2,6,1024,128]{2,3,1,0:T(8,128)(2,1)}) %all-gather.7.cloned.1.call-update) | async-done | bytes 3145744 | tf_op jit(solution)/shard_map/all_gather | solution.py:48
  275.9 5.6 %multiply_reduce_fusion.2 = (f32[2]{0:T(128)S(1)}, f32[2,384,6,128]{1,3,2,0:T(8,128)}) fusion(bf16[2,6,1024,128]{2,3,1,0:T(8,128)(2,1)} %all-gather.7.cloned.1.call-done, bf16[2,1024,384,1]{2,1,3,0:T(8,128)(2,1)} %bitcast.75), kind=kOutput, calls=%fused_computation.5 | convolution fusion | flops 1209139200 | bytes 7077896 | tf_op jit(solution)/shard_map/ipe,ihpd->iehd/dot_general | solution.py:54
  281.5 38.5 %psum.7 = f32[2]{0:T(128)S(1)} all-reduce(f32[2]{0:T(128)S(1)} %add.30), channel_id=1, replica_groups=mesh['seq'=8,'tensor'=4] {'seq','tensor'}, use_global_device_ids=true, to_apply=%region_5.0 | all-reduce | flops 2 | bytes 16 | tf_op jit(solution)/shard_map/psum | solution.py:61
  320.6 2.6 slice_multiply_fusion.1
  323.2 1.5 slice_multiply_fusion.3
  324.7 1.4 copy.41
  326.1 1.4 copy.42
  327.5 2.7 fusion
  330.2 1.2 add_multiply_fusion
  (41 shorter events, 5.5 us)
Async XLA Ops:
  7.2 46.8 %all-gather.5.cloned.1.call-start = ((), (), s32[]{:S(2)}) async-start(), calls=%async_computation.3 | async-start | bytes 3538944 | tf_op jit(solution)/shard_map/all_gather | solution.py:31
  7.2 5.7 %copy-start.6 = (bf16[2,128,3072]{2,1,0:T(8,128)(2,1)S(1)}, bf16[2,128,3072]{2,1,0:T(8,128)(2,1)}, u32[]{:S(2)}) copy-start(bf16[2,128,3072]{2,1,0:T(8,128)(2,1)} %param.8) | copy-start | bytes 4718596
  12.8 80.5 %all-gather.9.cloned.1.call-start = ((), (), s32[]{:S(2)}) async-start(), calls=%async_computation.5 | async-start | bytes 3538944 | tf_op jit(solution)/shard_map/all_gather | solution.py:33
  17.9 4.4 %copy-start.5 = (bf16[2,128,3072]{2,1,0:T(8,128)(2,1)S(1)}, bf16[2,128,3072]{2,1,0:T(8,128)(2,1)}, u32[]{:S(2)}) copy-start(bf16[2,128,3072]{2,1,0:T(8,128)(2,1)} %param.13) | copy-start | bytes 4718596
  17.9 140.3 %reduce-scatter.4.cloned.1.call-start = ((), (), s32[]{:S(2)}) async-start(), calls=%async_computation.7 | async-start | bytes 3538944
  57.0 2.7 copy-start
  73.3 169.2 %all-gather.11.cloned.1.call-start = ((), (), s32[]{:S(2)}) async-start(), calls=%async_computation.6 | async-start | bytes 3538944 | tf_op jit(solution)/shard_map/all_gather | solution.py:52
  102.1 63.7 %all-to-all-start.1 = ((bf16[2,128,3072]{1,0,2:T(2,128)(2,1)}), bf16[2,128,3072]{1,0,2:T(2,128)(2,1)S(1)}, u32[]{:S(2)}, u32[]{:S(2)}) async-start(bf16[2,128,3072]{1,0,2:T(2,128)(2,1)} %copy.38), calls=%async_computation.1 | async-start | bytes 3145728 | tf_op jit(solution)/shard_map/all_to_all | solution.py:20
  105.6 170.3 %all-gather.7.cloned.1.call-start = ((), (), s32[]{:S(2)}) async-start(), calls=%async_computation.4 | async-start | bytes 3538944 | tf_op jit(solution)/shard_map/all_gather | solution.py:48
  165.7 73.8 %all-to-all-start = ((bf16[2,128,3072]{1,0,2:T(2,128)(2,1)}), bf16[2,128,3072]{1,0,2:T(2,128)(2,1)S(1)}, u32[]{:S(2)}, u32[]{:S(2)}) async-start(bf16[2,128,3072]{1,0,2:T(2,128)(2,1)} %copy.34), calls=%async_computation | async-start | bytes 3145728 | tf_op jit(solution)/shard_map/all_to_all | solution.py:19
  320.6 2.6 copy-start.4
  326.1 1.4 copy-start.1
  327.5 2.7 copy-start.2
  327.5 2.7 copy-start.3
  327.5 2.7 copy-start.7
Sparse Core Ops, SparseCore 0:
  12.9 40.9 all-gather.4
  56.1 37.1 all-gather.8
  95.6 62.5 reduce-scatter.3
  160.2 75.7 all-gather.10
  238.1 37.8 all-gather.6

commit v2 on v1

--- a/solution.py
+++ b/solution.py
@@ -1,14 +1,17 @@
+import functools
 import math
 
 import jax
 import jax.numpy as jnp
 from jax import lax
+from jax.experimental import pallas as pl
+from jax.experimental.pallas import tpu as pltpu
 from jax.sharding import PartitionSpec as P
 
 HEAD_DIM = 128
 
 
-def local(tokens, w_query, w_key, w_value, w_out, cotangent, noise_value, noise_out):
+def local_general(tokens, w_query, w_key, w_value, w_out, cotangent, noise_value, noise_out):
     images, patch_rows, width = tokens.shape
     columns = w_query.shape[1]
     head_count = columns // HEAD_DIM
@@ -68,6 +71,418 @@
     return (grad_value / images, grad_out / images)
 
 
+MESH = pl.DeviceIdType.MESH
+F32 = jnp.float32
+BF16 = jnp.bfloat16
+ROWS_DOT = (((1,), (1,)), ((), ()))
+DEPTH_DOT = (((0,), (0,)), ((), ()))
+
+
+def fused_kernel(
+    n_seq, n_ten, tok_h, cot_h, wq_h, wk_h, wv_h, wo_h, nv_h, no_h, gv, go,
+    tok, cot, w3, wo, loc, recv, tmp, gath, cols, cols_t, acc, nv, no, dv_t, sq_seq, sq_ten,
+    in_sem, w_sem, own_sem, a2a_s, a2a_r, tk_s, tk_r, fw_s, fw_r,
+    ag_s, ag_r, sib_s, sib_r, sq_s, sq_r, st_s, st_r,
+):
+    me = lax.axis_index("seq")
+    ten = lax.axis_index("tensor")
+    chip, core = me // 2, me % 2
+    n_chip = n_seq // 2
+    sibling = 2 * chip + 1 - core
+    rows = tok.shape[0]
+    patch = rows // 2
+    width = tok.shape[1]
+    block = width // n_seq
+    quarter = rows // n_ten
+    patches = patch * n_seq
+    half = patches // 2
+    score_scale = 1.0 / math.sqrt(HEAD_DIM)
+
+    loads = [
+        pltpu.make_async_copy(tok_h, tok, in_sem.at[0]),
+        pltpu.make_async_copy(wk_h, w3.at[0], w_sem.at[0]),
+        pltpu.make_async_copy(wq_h, w3.at[1], w_sem.at[1]),
+        pltpu.make_async_copy(wv_h, w3.at[2], w_sem.at[2]),
+        pltpu.make_async_copy(cot_h, cot, in_sem.at[1]),
+        pltpu.make_async_copy(wo_h, wo, w_sem.at[3]),
+        pltpu.make_async_copy(nv_h, nv, in_sem.at[2]),
+        pltpu.make_async_copy(no_h, no, in_sem.at[3]),
+    ]
+    for load in loads:
+        load.start()
+
+    barrier = pltpu.get_barrier_semaphore()
+    for step in range(1, n_seq):
+        pl.semaphore_signal(
+            barrier, inc=1, device_id=((me + step) % n_seq, ten), device_id_type=MESH
+        )
+    for step in range(1, n_ten):
+        pl.semaphore_signal(
+            barrier, inc=1, device_id=(me, (ten + step) % n_ten), device_id_type=MESH
+        )
+    pl.semaphore_wait(barrier, n_seq + n_ten - 2)
+
+    def remote(source, target, send_sem, recv_sem, seq_at, ten_at):
+        return pltpu.make_async_remote_copy(
+            src_ref=source, dst_ref=target, send_sem=send_sem, recv_sem=recv_sem,
+            device_id=(seq_at, ten_at), device_id_type=MESH,
+        )
+
+    def first_head(device):
+        return 3 * ((device // 2) % 2) + device % 2
+
+    def image_of(device):
+        return device // 4
+
+    def head_rows(device):
+        return pl.ds(pl.multiple_of(device * patch, patch), patch)
+
+    def exchange(kind, step, source):
+        peer = (me + step) % n_seq
+        if source:
+            peer = (me + n_seq - step) % n_seq
+        sender, target = (peer, me) if source else (me, peer)
+        return remote(
+            loc.at[kind, pl.ds(first_head(target), 2),
+                   pl.ds(pl.multiple_of(image_of(target) * patch, patch), patch)],
+            recv.at[kind, :, head_rows(sender)],
+            a2a_s.at[kind, step], a2a_r.at[kind, step], peer, ten,
+        )
+
+    def send_heads(kind):
+        @pl.loop(1, n_seq)
+        def _(step):
+            exchange(kind, step, False).start()
+
+        recv[kind, :, head_rows(me), :] = loc[
+            kind, pl.ds(first_head(me), 2),
+            pl.ds(pl.multiple_of(image_of(me) * patch, patch), patch), :
+        ]
+
+    def project(kind):
+        @pl.loop(0, 3)
+        def _(at):
+            chunk = pl.ds(pl.multiple_of(at * 256, 256), 256)
+            if kind < 3:
+                out = jnp.dot(tok[...], w3[kind, :, chunk], preferred_element_type=F32)
+            else:
+                out = lax.dot_general(cot[...], wo[chunk, :], ROWS_DOT, preferred_element_type=F32)
+            out = out.astype(BF16)
+            loc[kind, 2 * at] = out[:, :HEAD_DIM]
+            loc[kind, 2 * at + 1] = out[:, HEAD_DIM:]
+
+    loads[0].wait()
+    for kind in range(3):
+        loads[1 + kind].wait()
+        project(kind)
+        send_heads(kind)
+    loads[4].wait()
+    loads[5].wait()
+    project(3)
+    send_heads(3)
+
+    held = (tok, cot)
+
+    def own_columns(which):
+        return pltpu.make_async_copy(
+            held[which].at[:, pl.ds(pl.multiple_of(me * block, block), block)],
+            cols.at[which, me], own_sem.at[which],
+        )
+
+    def ten_rows(index):
+        return pl.ds(pl.multiple_of(index * quarter, quarter), quarter)
+
+    def column_copy(which, step, source):
+        peer = (me + step) % n_seq
+        if source:
+            peer = (me + n_seq - step) % n_seq
+        sender, target = (peer, me) if source else (me, peer)
+        return remote(
+            held[which].at[ten_rows(ten), pl.ds(pl.multiple_of(target * block, block), block)],
+            cols.at[which, sender, ten_rows(ten), :],
+            tk_s.at[which, step], tk_r.at[which, step], peer, ten,
+        )
+
+    def column_share(which, step, hop, source):
+        origin = (me + n_seq - step) % n_seq
+        peer = (ten + hop) % n_ten
+        if source:
+            peer = (ten + n_ten - hop) % n_ten
+        piece = cols.at[which, origin, ten_rows(peer if source else ten), :]
+        return remote(
+            piece, piece, fw_s.at[which, step, hop], fw_r.at[which, step, hop], me, peer
+        )
+
+    for which in range(2):
+        own_columns(which).start()
+
+        @pl.loop(1, n_seq)
+        def _(step):
+            column_copy(which, step, False).start()
+
+    for kind in range(4):
+        @pl.loop(1, n_seq)
+        def _(step):
+            exchange(kind, step, True).wait_recv()
+
+    @pl.loop(0, 2)
+    def _(slot):
+        dv_t[...] = jnp.zeros_like(dv_t)
+
+        @pl.loop(0, patches // 256)
+        def _(at):
+            part = pl.ds(pl.multiple_of(at * 256, 256), 256)
+            scores = lax.dot_general(
+                recv[1, slot, part, :], recv[0, slot], ROWS_DOT, preferred_element_type=F32
+            ) * score_scale
+            top = jnp.max(scores, axis=1, keepdims=True)
+            raised = jnp.exp(scores - top)
+            total = jnp.sum(raised, axis=1, keepdims=True)
+            probs = (raised * (1.0 / total)).astype(BF16)
+            attended = jnp.dot(probs, recv[2, slot], preferred_element_type=F32)
+            tmp[0, slot, part, :] = attended.astype(BF16)
+            dv_t[...] += lax.dot_general(
+                recv[3, slot, part, :], probs, DEPTH_DOT, preferred_element_type=F32
+            )
+
+        tmp[1, slot] = dv_t[...].T.astype(BF16)
+
+    def own_head(at_chip, at_core):
+        return (at_chip // 2) * 6 + 3 * (at_chip % 2) + 2 * at_core
+
+    def shared_head(at_chip):
+        return (at_chip // 2) * 6 + 3 * (at_chip % 2) + 1
+
+    def half_rows(at_core):
+        return pl.ds(pl.multiple_of(at_core * half, half), half)
+
+    def place(which, part, at_chip, at_core):
+        if part == 0:
+            return gath.at[which, own_head(at_chip, at_core)]
+        return gath.at[which, shared_head(at_chip), half_rows(at_core), :]
+
+    def made(which, part):
+        if part == 0:
+            return tmp.at[which, core]
+        return tmp.at[which, 1 - core, half_rows(core), :]
+
+    def plane_copy(which, part, step, source):
+        other = (chip + step) % n_chip
+        if source:
+            other = (chip + n_chip - step) % n_chip
+        return remote(
+            made(which, part), place(which, part, other if source else chip, core),
+            ag_s.at[which, part, step], ag_r.at[which, part, step], 2 * other + core, ten,
+        )
+
+    def sibling_copy(which, part, step, source):
+        origin = (chip + n_chip - step) % n_chip
+        piece = place(which, part, origin, 1 - core if source else core)
+        return remote(
+            piece, piece, sib_s.at[which, part, step], sib_r.at[which, part, step], sibling, ten
+        )
+
+    for which in range(2):
+        for part in range(2):
+            @pl.loop(1, n_chip)
+            def _(step):
+                plane_copy(which, part, step, False).start()
+
+        gath[which, own_head(chip, core)] = tmp[which, core]
+        gath[which, shared_head(chip), half_rows(core), :] = tmp[
+            which, 1 - core, half_rows(core), :
+        ]
+        for part in range(2):
+            sibling_copy(which, part, 0, False).start()
+
+    for which in range(2):
+        @pl.loop(1, n_seq)
+        def _(step):
+            column_copy(which, step, True).wait_recv()
+
+            @pl.loop(1, n_ten)
+            def _(hop):
+                column_share(which, step, hop, False).start()
+
+        own_columns(which).wait()
+
+    for which in range(2):
+        @pl.loop(1, n_seq)
+        def _(step):
+            @pl.loop(1, n_ten)
+            def _(hop):
+                column_share(which, step, hop, True).wait_recv()
+
+        @pl.loop(0, n_seq)
+        def _(origin):
+            lanes = pl.ds(pl.multiple_of(origin * patch, patch), patch)
+            for image in range(2):
+                piece = cols[which, origin, image * patch:(image + 1) * patch, :]
+                cols_t[which, image, :, lanes] = piece.T
+
+    for which in range(2):
+        @pl.loop(1, n_chip)
+        def _(step):
+            for part in range(2):
+                plane_copy(which, part, step, True).wait_recv()
+                sibling_copy(which, part, step, False).start()
+
+    squares = [jnp.zeros((1, 256), F32), jnp.zeros((1, 256), F32)]
+    for which in range(2):
+        @pl.loop(0, n_chip)
+        def _(step):
+            for part in range(2):
+                sibling_copy(which, part, step, True).wait_recv()
+
+        for image in range(2):
+            for at in range(3):
+                head = image * 6 + 2 * at
+                heads = jnp.concatenate([gath[which, head], gath[which, head + 1]], axis=1)
+                product = jnp.dot(
+                    cols_t[1 - which, image], heads, preferred_element_type=F32
+                )
+                acc[which, image, :, at * 256:(at + 1) * 256] = product
+                squares[image] += jnp.sum(product * product, axis=0, keepdims=True)
+
+    def spread(value):
+        return jnp.broadcast_to(jnp.sum(value, axis=1, keepdims=True), (8, HEAD_DIM))
+
+    sq_seq[me, 0:8, :] = spread(squares[0])
+    sq_seq[me, 8:16, :] = spread(squares[1])
+
+    def square_seq(step, source):
+        peer = (me + step) % n_seq
+        if source:
+            peer = (me + n_seq - step) % n_seq
+        piece = sq_seq.at[peer if source else me]
+        return remote(piece, piece, sq_s.at[step], sq_r.at[step], peer, ten)
+
+    def square_ten(step, source):
+        peer = (ten + step) % n_ten
+        if source:
+            peer = (ten + n_ten - step) % n_ten
+        piece = sq_ten.at[peer if source else ten]
+        return remote(piece, piece, st_s.at[step], st_r.at[step], me, peer)
+
+    for step in range(1, n_seq):
+        square_seq(step, False).start()
+    for step in range(1, n_seq):
+        square_seq(step, True).wait_recv()
+    sq_ten[ten] = jnp.sum(sq_seq[...], axis=0)
+    for step in range(1, n_ten):
+        square_ten(step, False).start()
+    loads[6].wait()
+    loads[7].wait()
+    for step in range(1, n_ten):
+        square_ten(step, True).wait_recv()
+    norm = jnp.sum(sq_ten[...], axis=0)
+    factor = math.sqrt(2.0 * width * width) / (jnp.sqrt(norm) + 0.01)
+    first, second = factor[0:1, 0:1], factor[8:9, 0:1]
+
+    @pl.loop(0, 6)
+    def _(at):
+        lanes = pl.ds(pl.multiple_of(at * HEAD_DIM, HEAD_DIM), HEAD_DIM)
+        value = nv[:, lanes] + first * acc[1, 0, :, lanes] + second * acc[1, 1, :, lanes]
+        gv[:, lanes] = value * 0.5
+        mixed = first * acc[0, 0, :, lanes] + second * acc[0, 1, :, lanes]
+        go[lanes, :] = (no[lanes, :] + mixed.T) * 0.5
+
+    for kind in range(4):
+        @pl.loop(1, n_seq)
+        def _(step):
+            exchange(kind, step, False).wait_send()
+    for which in range(2):
+        @pl.loop(1, n_seq)
+        def _(step):
+            column_copy(which, step, False).wait_send()
+
+            @pl.loop(1, n_ten)
+            def _(hop):
+                column_share(which, step, hop, False).wait_send()
+
+        for part in range(2):
+            @pl.loop(1, n_chip)
+            def _(step):
+                plane_copy(which, part, step, False).wait_send()
+
+            @pl.loop(0, n_chip)
+            def _(step):
+                sibling_copy(which, part, step, False).wait_send()
+    for step in range(1, n_seq):
+        square_seq(step, False).wait_send()
+    for step in range(1, n_ten):
+        square_ten(step, False).wait_send()
+
+
+def local_fused(
+    n_seq, n_ten, tokens, w_query, w_key, w_value, w_out, cotangent, noise_value, noise_out
+):
+    images, patch, width = tokens.shape
+    columns = w_query.shape[1]
+    rows, patches, block = images * patch, patch * n_seq, width // n_seq
+    n_chip = n_seq // 2
+    dma = pltpu.SemaphoreType.DMA
+    return pl.pallas_call(
+        functools.partial(fused_kernel, n_seq, n_ten),
+        out_shape=(
+            jax.ShapeDtypeStruct(noise_value.shape, F32),
+            jax.ShapeDtypeStruct(noise_out.shape, F32),
+        ),
+        in_specs=[pl.BlockSpec(memory_space=pl.ANY)] * 8,
+        out_specs=[pl.BlockSpec(memory_space=pltpu.VMEM)] * 2,
+        scratch_shapes=[
+            pltpu.VMEM((rows, width), BF16),
+            pltpu.VMEM((rows, width), BF16),
+            pltpu.VMEM((3, width, columns), BF16),
+            pltpu.VMEM((columns, width), BF16),
+            pltpu.VMEM((4, 6, rows, HEAD_DIM), BF16),
+            pltpu.VMEM((4, 2, patches, HEAD_DIM), BF16),
+            pltpu.VMEM((2, 2, patches, HEAD_DIM), BF16),
+            pltpu.VMEM((2, 12, patches, HEAD_DIM), BF16),
+            pltpu.VMEM((2, n_seq, rows, block), BF16),
+            pltpu.VMEM((2, 2, block, patches), BF16),
+            pltpu.VMEM((2, 2, block, columns), F32),
+            pltpu.VMEM(noise_value.shape, F32),
+            pltpu.VMEM(noise_out.shape, F32),
+            pltpu.VMEM((HEAD_DIM, patches), F32),
+            pltpu.VMEM((n_seq, 16, HEAD_DIM), F32),
+            pltpu.VMEM((n_ten, 16, HEAD_DIM), F32),
+            dma((4,)),
+            dma((4,)),
+            dma((2,)),
+            dma((4, n_seq)),
+            dma((4, n_seq)),
+            dma((2, n_seq)),
+            dma((2, n_seq)),
+            dma((2, n_seq, n_ten)),
+            dma((2, n_seq, n_ten)),
+            dma((2, 2, n_chip)),
+            dma((2, 2, n_chip)),
+            dma((2, 2, n_chip)),
+            dma((2, 2, n_chip)),
+            dma((n_seq,)),
+            dma((n_seq,)),
+            dma((n_ten,)),
+            dma((n_ten,)),
+        ],
+        compiler_params=pltpu.CompilerParams(
+            collective_id=0, has_side_effects=True, vmem_limit_bytes=60 * 1024 * 1024
+        ),
+    )(
+        tokens.reshape(rows, width), cotangent.reshape(rows, width),
+        w_query, w_key, w_value, w_out, noise_value, noise_out,
+    )
+
+
+def local(n_seq, n_ten, *arrays):
+    images, patch, width = arrays[0].shape
+    heads = arrays[1].shape[1] // HEAD_DIM
+    fits = n_seq == 8 and n_ten == 4 and images == 2 and heads == 6 and patch == 128
+    if fits and width == 3072:
+        return local_fused(n_seq, n_ten, *arrays)
+    return local_general(*arrays)
+
+
 def solution(mesh):
     placed = (
         P(None, "seq", None),
@@ -80,7 +495,7 @@
         P("tensor", "seq"),
     )
     return jax.shard_map(
-        local,
+        functools.partial(local, mesh.shape["seq"], mesh.shape["tensor"]),
         mesh=mesh,
         in_specs=placed,
         out_specs=(P("seq", "tensor"), P("tensor", "seq")),

time: 339 us -> 161 us (0.47)
  waiting for transfers between devices: 187 us -> 0 us
  Pallas kernels: 0 us -> 156 us
  blocking collectives: 38.5 us -> 0 us
  matrix products: 36.9 us -> 0 us
  local copies, waits for them, and re-layouts: 36 us -> 3.47 us
  starting transfers between devices: 16.7 us -> 0 us
  between operations: 13.9 us -> 0.65 us
  other arithmetic: 9.29 us -> 0 us
    pallas_call x0 -> x1, Pallas kernels: none -> 156 us  [local_fused(): pl.pallas_call(functools.partial(fused_kernel, n_seq, n_ten), out_shape=(...]
    all_gather x4 -> x0, waiting for transfers between devices: 76 us -> none  [the longest x1 28.8 us: local(): d_value_all = lax.all_gather(d_value, 'seq', axis=2, tiled=True)]
    all_to_all x2 -> x0, waiting for transfers between devices: 58.3 us -> none  [the longest x1 58.3 us: local(): lax.all_to_all(tokens, 'seq', split_axis=2, concat_axis=1, tiled=True)]
    unnamed x6 -> x0, waiting for transfers between devices: 52.3 us -> none
    psum x1 -> x0, blocking collectives: 38.5 us -> none  [local(): squares = lax.psum(partial, ('seq', 'tensor'))]
    dot_general x9 -> x0, matrix products: 36.9 us -> none  [the longest x3 11.9 us: project(): product = jnp.dot(flat_tokens, weight, preferred_element_type=jnp.float32)]
    unnamed x22 -> x4, local copies, waits for them, and re-layouts: 23.5 us -> 3.47 us
    all_to_all x2 -> x0, starting transfers between devices: 16.1 us -> none  [the longest x1 12.5 us: local(): lax.all_to_all(tokens, 'seq', split_axis=2, concat_axis=1, tiled=True)]
  transfers between devices with their start and end apart: 7 -> 0, of which waited for: 5 -> 0; matrix products, arithmetic and copies ran while one was open for 17% -> 0% of each run, Pallas kernels for 0% -> 0%
where the time goes in v2:
time: 161 us
  Pallas kernels  156 us (97%)
  local copies, waits for them, and re-layouts  3.47 us (2%)
    pallas_call x1, Pallas kernels, local_fused(): pl.pallas_call(functools.partial(fused_kernel, n_seq, n_ten), out_shape=(...  156 us
    unnamed x4, local copies, waits for them, and re-layouts  3.47 us

profile of v2, /device:TPU:0, one launch (start us, length us, event | category | flops | bytes accessed | tf_op | source)
XLA Modules:
  0.0 160.6 jit_solution(289057924801375154)
XLA Ops:
  0.6 156.5 %shard_map.95 = (f32[384,768]{1,0:T(8,128)}, f32[768,384]{1,0:T(8,128)}) custom-call(bf16[256,3072]{1,0:T(8,128)(2,1)} %bitcast.2, bf16[256,3072]{1,0:T(8,128)(2,1)} %bitcast.3, bf16[3072,768]{1,0:T(8,128)(2,1)} %wq_h.1, bf16[3072,768]{1,0:T(8,128)(2,1)} %wk_h.1, bf16[3072,768]{1,0:T(8,128)(2,1)} %wv_h.1, bf16[768,3072]{1,0:T(8,128)(2,1)} %wo_h.1, ...), custom_call_target="tpu_custom_call" | custom-call | tf_op jit(solution)/shard_map/pallas_call | solution.py:425
  157.1 0.0 copy-start
  157.1 2.5 %copy.12 = f32[384,768]{1,0:T(8,128)} copy(f32[384,768]{1,0:T(8,128)} %get-tuple-element.4) | data formatting | bytes 2359296
  159.6 0.0 copy-done
  159.6 1.0 copy.13
Async XLA Ops:
  157.1 2.5 %copy-start = (f32[768,384]{1,0:T(8,128)S(1)}, f32[768,384]{1,0:T(8,128)}, u32[]{:S(2)}) copy-start(f32[768,384]{1,0:T(8,128)} %get-tuple-element.5) | copy-start | bytes 3538948

commit v3 on v2

--- a/solution.py
+++ b/solution.py
@@ -80,8 +80,8 @@
 
 def fused_kernel(
     n_seq, n_ten, tok_h, cot_h, wq_h, wk_h, wv_h, wo_h, nv_h, no_h, gv, go,
-    tok, cot, w3, wo, loc, recv, tmp, gath, cols, cols_t, acc, nv, no, dv_t, sq_seq, sq_ten,
-    in_sem, w_sem, own_sem, a2a_s, a2a_r, tk_s, tk_r, fw_s, fw_r,
+    tok, cot, w3, wo, loc, recv, tmp, gath, cols, cols_t, acc, nv, no, probs, sq_seq, sq_ten,
+    in_sem, w_sem, own_sem, a2a_s, a2a_r, hs_s, hs_r, tk_s, tk_r, fw_s, fw_r,
     ag_s, ag_r, sib_s, sib_r, sq_s, sq_r, st_s, st_r,
 ):
     me = lax.axis_index("seq")
@@ -128,36 +128,54 @@
             device_id=(seq_at, ten_at), device_id_type=MESH,
         )
 
-    def first_head(device):
-        return 3 * ((device // 2) % 2) + device % 2
-
-    def image_of(device):
-        return device // 4
-
     def head_rows(device):
         return pl.ds(pl.multiple_of(device * patch, patch), patch)
 
+    def chip_heads(kind, at_chip):
+        image = at_chip // 2
+        return loc.at[
+            kind, pl.ds(3 * (at_chip % 2), 3), pl.ds(pl.multiple_of(image * patch, patch), patch)
+        ]
+
     def exchange(kind, step, source):
-        peer = (me + step) % n_seq
+        other = (chip + step) % n_chip
         if source:
-            peer = (me + n_seq - step) % n_seq
-        sender, target = (peer, me) if source else (me, peer)
+            other = (chip + n_chip - step) % n_chip
+        peer = 2 * other + core
         return remote(
-            loc.at[kind, pl.ds(first_head(target), 2),
-                   pl.ds(pl.multiple_of(image_of(target) * patch, patch), patch)],
-            recv.at[kind, :, head_rows(sender)],
+            chip_heads(kind, other), recv.at[kind, :, head_rows(peer if source else me)],
             a2a_s.at[kind, step], a2a_r.at[kind, step], peer, ten,
         )
 
+    def pass_heads(kind, step, source):
+        origin = 2 * ((chip + n_chip - step) % n_chip)
+        to_core = core if source else 1 - core
+        piece = recv.at[kind, pl.ds(to_core, 2), head_rows(origin + 1 - to_core)]
+        return remote(
+            piece, piece, hs_s.at[kind, step], hs_r.at[kind, step], sibling, ten
+        )
+
     def send_heads(kind):
-        @pl.loop(1, n_seq)
+        @pl.loop(1, n_chip)
         def _(step):
             exchange(kind, step, False).start()
 
         recv[kind, :, head_rows(me), :] = loc[
-            kind, pl.ds(first_head(me), 2),
-            pl.ds(pl.multiple_of(image_of(me) * patch, patch), patch), :
+            kind, pl.ds(3 * (chip % 2), 3),
+            pl.ds(pl.multiple_of((chip // 2) * patch, patch), patch), :
         ]
+        pass_heads(kind, 0, False).start()
+
+    def pass_on(kind):
+        @pl.loop(1, n_chip)
+        def _(step):
+            exchange(kind, step, True).wait_recv()
+            pass_heads(kind, step, False).start()
+
+    def have_heads(kind):
+        @pl.loop(0, n_chip)
+        def _(step):
+            pass_heads(kind, step, True).wait_recv()
 
     def project(kind):
         @pl.loop(0, 3)
@@ -171,16 +189,6 @@
             loc[kind, 2 * at] = out[:, :HEAD_DIM]
             loc[kind, 2 * at + 1] = out[:, HEAD_DIM:]
 
-    loads[0].wait()
-    for kind in range(3):
-        loads[1 + kind].wait()
-        project(kind)
-        send_heads(kind)
-    loads[4].wait()
-    loads[5].wait()
-    project(3)
-    send_heads(3)
-
     held = (tok, cot)
 
     def own_columns(which):
@@ -213,39 +221,57 @@
             piece, piece, fw_s.at[which, step, hop], fw_r.at[which, step, hop], me, peer
         )
 
-    for which in range(2):
+    def send_columns(which):
         own_columns(which).start()
 
         @pl.loop(1, n_seq)
         def _(step):
             column_copy(which, step, False).start()
 
-    for kind in range(4):
+    def share_columns(which):
         @pl.loop(1, n_seq)
         def _(step):
-            exchange(kind, step, True).wait_recv()
+            column_copy(which, step, True).wait_recv()
+
+            @pl.loop(1, n_ten)
+            def _(hop):
+                column_share(which, step, hop, False).start()
+
+        own_columns(which).wait()
+
+    loads[0].wait()
+    send_columns(0)
+    for kind in range(3):
+        loads[1 + kind].wait()
+        project(kind)
+        send_heads(kind)
+    loads[4].wait()
+    loads[5].wait()
+    project(3)
+    send_heads(3)
+
+    send_columns(1)
+    pass_on(0)
+    pass_on(1)
+    have_heads(0)
+    have_heads(1)
+    blocks = patches // 256
+
+    def strip(at):
+        return pl.ds(pl.multiple_of(at * 256, 256), 256)
 
     @pl.loop(0, 2)
     def _(slot):
-        dv_t[...] = jnp.zeros_like(dv_t)
-
-        @pl.loop(0, patches // 256)
+        @pl.loop(0, blocks)
         def _(at):
-            part = pl.ds(pl.multiple_of(at * 256, 256), 256)
             scores = lax.dot_general(
-                recv[1, slot, part, :], recv[0, slot], ROWS_DOT, preferred_element_type=F32
+                recv[1, core + slot, strip(at), :], recv[0, core + slot], ROWS_DOT,
+                preferred_element_type=F32,
             ) * score_scale
             top = jnp.max(scores, axis=1, keepdims=True)
             raised = jnp.exp(scores - top)
             total = jnp.sum(raised, axis=1, keepdims=True)
-            probs = (raised * (1.0 / total)).astype(BF16)
-            attended = jnp.dot(probs, recv[2, slot], preferred_element_type=F32)
-            tmp[0, slot, part, :] = attended.astype(BF16)
-            dv_t[...] += lax.dot_general(
-                recv[3, slot, part, :], probs, DEPTH_DOT, preferred_element_type=F32
-            )
-
-        tmp[1, slot] = dv_t[...].T.astype(BF16)
+            probs[slot, strip(at), :] = (raised * (1.0 / total)).astype(BF16)
 
     def own_head(at_chip, at_core):
         return (at_chip // 2) * 6 + 3 * (at_chip % 2) + 2 * at_core
@@ -282,7 +308,7 @@
             piece, piece, sib_s.at[which, part, step], sib_r.at[which, part, step], sibling, ten
         )
 
-    for which in range(2):
+    def send_results(which):
         for part in range(2):
             @pl.loop(1, n_chip)
             def _(step):
@@ -295,18 +321,37 @@
         for part in range(2):
             sibling_copy(which, part, 0, False).start()
 
-    for which in range(2):
-        @pl.loop(1, n_seq)
-        def _(step):
-            column_copy(which, step, True).wait_recv()
-
-            @pl.loop(1, n_ten)
-            def _(hop):
-                column_share(which, step, hop, False).start()
-
-        own_columns(which).wait()
-
-    for which in range(2):
+    pass_on(2)
+    have_heads(2)
+
+    @pl.loop(0, 2)
+    def _(slot):
+        @pl.loop(0, blocks)
+        def _(at):
+            attended = jnp.dot(
+                probs[slot, strip(at), :], recv[2, core + slot], preferred_element_type=F32
+            )
+            tmp[0, slot, strip(at), :] = attended.astype(BF16)
+
+    send_results(0)
+    pass_on(3)
+    have_heads(3)
+
+    @pl.loop(0, 2)
+    def _(slot):
+        @pl.loop(0, blocks)
+        def _(at):
+            d_value = lax.dot_general(
+                recv[3, core + slot], probs[slot, :, strip(at)], DEPTH_DOT,
+                preferred_element_type=F32,
+            )
+            tmp[1, slot, strip(at), :] = d_value.T.astype(BF16)
+
+    send_results(1)
+    share_columns(0)
+    share_columns(1)
+
+    def turn_columns(which):
         @pl.loop(1, n_seq)
         def _(step):
             @pl.loop(1, n_ten)
@@ -320,35 +365,55 @@
                 piece = cols[which, origin, image * patch:(image + 1) * patch, :]
                 cols_t[which, image, :, lanes] = piece.T
 
-    for which in range(2):
-        @pl.loop(1, n_chip)
-        def _(step):
-            for part in range(2):
-                plane_copy(which, part, step, True).wait_recv()
-                sibling_copy(which, part, step, False).start()
-
-    squares = [jnp.zeros((1, 256), F32), jnp.zeros((1, 256), F32)]
-    for which in range(2):
-        @pl.loop(0, n_chip)
-        def _(step):
-            for part in range(2):
-                sibling_copy(which, part, step, True).wait_recv()
-
-        for image in range(2):
-            for at in range(3):
-                head = image * 6 + 2 * at
-                heads = jnp.concatenate([gath[which, head], gath[which, head + 1]], axis=1)
-                product = jnp.dot(
-                    cols_t[1 - which, image], heads, preferred_element_type=F32
-                )
-                acc[which, image, :, at * 256:(at + 1) * 256] = product
-                squares[image] += jnp.sum(product * product, axis=0, keepdims=True)
-
-    def spread(value):
-        return jnp.broadcast_to(jnp.sum(value, axis=1, keepdims=True), (8, HEAD_DIM))
-
-    sq_seq[me, 0:8, :] = spread(squares[0])
-    sq_seq[me, 8:16, :] = spread(squares[1])
+    near = chip // 2
+    partner = chip + 1 - 2 * (chip % 2)
+    partner_step = (chip + n_chip - partner) % n_chip
+    far_steps = [
+        (chip + n_chip - (2 * (1 - near) + at)) % n_chip for at in range(2)
+    ]
+
+    def pass_results(which, step):
+        for part in range(2):
+            plane_copy(which, part, step, True).wait_recv()
+            sibling_copy(which, part, step, False).start()
+
+    def have_results(which, step):
+        for part in range(2):
+            sibling_copy(which, part, step, True).wait_recv()
+
+    def multiply(which, image):
+        @pl.loop(0, 3)
+        def _(at):
+            head = image * 6 + 2 * at
+            heads = jnp.concatenate([gath[which, head], gath[which, head + 1]], axis=1)
+            product = jnp.dot(cols_t[1 - which, image], heads, preferred_element_type=F32)
+            acc[which, image, at] = product
+            folded = jnp.sum((product * product).reshape(-1, 8, 256), axis=0)
+            sq_seq[me, pl.ds(pl.multiple_of(image * 8, 8), 8), :] += (
+                folded[:, :HEAD_DIM] + folded[:, HEAD_DIM:]
+            )
+
+    sq_seq[me] = jnp.zeros((16, HEAD_DIM), F32)
+    pass_results(0, partner_step)
+    turn_columns(1)
+    pass_results(0, far_steps[0])
+    pass_results(0, far_steps[1])
+    pass_results(1, partner_step)
+    turn_columns(0)
+    have_results(0, 0)
+    have_results(0, partner_step)
+    multiply(0, near)
+    have_results(0, far_steps[0])
+    have_results(0, far_steps[1])
+    multiply(0, 1 - near)
+    have_results(1, 0)
+    have_results(1, partner_step)
+    multiply(1, near)
+    pass_results(1, far_steps[0])
+    pass_results(1, far_steps[1])
+    have_results(1, far_steps[0])
+    have_results(1, far_steps[1])
+    multiply(1, 1 - near)
 
     def square_seq(step, source):
         peer = (me + step) % n_seq
@@ -375,22 +440,27 @@
     loads[7].wait()
     for step in range(1, n_ten):
         square_ten(step, True).wait_recv()
-    norm = jnp.sum(sq_ten[...], axis=0)
+    total = jnp.sum(sq_ten[...], axis=0)
+    norm = jnp.sum(jnp.sum(total.reshape(2, 8, HEAD_DIM), axis=1), axis=1, keepdims=True)
     factor = math.sqrt(2.0 * width * width) / (jnp.sqrt(norm) + 0.01)
-    first, second = factor[0:1, 0:1], factor[8:9, 0:1]
-
-    @pl.loop(0, 6)
+    first, second = factor[0:1, :], factor[1:2, :]
+
+    @pl.loop(0, 3)
     def _(at):
-        lanes = pl.ds(pl.multiple_of(at * HEAD_DIM, HEAD_DIM), HEAD_DIM)
-        value = nv[:, lanes] + first * acc[1, 0, :, lanes] + second * acc[1, 1, :, lanes]
+        lanes = strip(at)
+        value = nv[:, lanes] + first * acc[1, 0, at] + second * acc[1, 1, at]
         gv[:, lanes] = value * 0.5
-        mixed = first * acc[0, 0, :, lanes] + second * acc[0, 1, :, lanes]
+        mixed = first * acc[0, 0, at] + second * acc[0, 1, at]
         go[lanes, :] = (no[lanes, :] + mixed.T) * 0.5
 
     for kind in range(4):
-        @pl.loop(1, n_seq)
+        @pl.loop(1, n_chip)
         def _(step):
             exchange(kind, step, False).wait_send()
+
+        @pl.loop(0, n_chip)
+        def _(step):
+            pass_heads(kind, step, False).wait_send()
     for which in range(2):
         @pl.loop(1, n_seq)
         def _(step):
@@ -436,22 +506,24 @@
             pltpu.VMEM((3, width, columns), BF16),
             pltpu.VMEM((columns, width), BF16),
             pltpu.VMEM((4, 6, rows, HEAD_DIM), BF16),
-            pltpu.VMEM((4, 2, patches, HEAD_DIM), BF16),
+            pltpu.VMEM((4, 3, patches, HEAD_DIM), BF16),
             pltpu.VMEM((2, 2, patches, HEAD_DIM), BF16),
             pltpu.VMEM((2, 12, patches, HEAD_DIM), BF16),
             pltpu.VMEM((2, n_seq, rows, block), BF16),
             pltpu.VMEM((2, 2, block, patches), BF16),
-            pltpu.VMEM((2, 2, block, columns), F32),
+            pltpu.VMEM((2, 2, 3, block, 256), F32),
             pltpu.VMEM(noise_value.shape, F32),
             pltpu.VMEM(noise_out.shape, F32),
-            pltpu.VMEM((HEAD_DIM, patches), F32),
+            pltpu.VMEM((2, patches, patches), BF16),
             pltpu.VMEM((n_seq, 16, HEAD_DIM), F32),
             pltpu.VMEM((n_ten, 16, HEAD_DIM), F32),
             dma((4,)),
             dma((4,)),
             dma((2,)),
-            dma((4, n_seq)),
-            dma((4, n_seq)),
+            dma((4, n_chip)),
+            dma((4, n_chip)),
+            dma((4, n_chip)),
+            dma((4, n_chip)),
             dma((2, n_seq)),
             dma((2, n_seq)),
             dma((2, n_seq, n_ten)),

time: 161 us -> 145 us (0.901)
  Pallas kernels: 156 us -> 141 us
    pallas_call x1, Pallas kernels: 156 us -> 141 us  [local_fused(): pl.pallas_call(functools.partial(fused_kernel, n_seq, n_ten), out_shape=(...]
where the time goes in v3:
time: 145 us
  Pallas kernels  141 us (97%)
  local copies, waits for them, and re-layouts  3.47 us (2%)
    pallas_call x1, Pallas kernels, local_fused(): pl.pallas_call(functools.partial(fused_kernel, n_seq, n_ten), out_shape=(...  141 us
    unnamed x4, local copies, waits for them, and re-layouts  3.47 us

profile of v3, /device:TPU:0, one launch (start us, length us, event | category | flops | bytes accessed | tf_op | source)
XLA Modules:
  0.0 144.9 jit_solution(14223529549875505501)
XLA Ops:
  0.6 140.8 %shard_map.95 = (f32[384,768]{1,0:T(8,128)}, f32[768,384]{1,0:T(8,128)}) custom-call(bf16[256,3072]{1,0:T(8,128)(2,1)} %bitcast.2, bf16[256,3072]{1,0:T(8,128)(2,1)} %bitcast.3, bf16[3072,768]{1,0:T(8,128)(2,1)} %wq_h.1, bf16[3072,768]{1,0:T(8,128)(2,1)} %wk_h.1, bf16[3072,768]{1,0:T(8,128)(2,1)} %wv_h.1, bf16[768,3072]{1,0:T(8,128)(2,1)} %wo_h.1, ...), custom_call_target="tpu_custom_call" | custom-call | tf_op jit(solution)/shard_map/pallas_call | solution.py:495
  141.5 0.0 copy-start
  141.5 2.5 %copy.12 = f32[384,768]{1,0:T(8,128)} copy(f32[384,768]{1,0:T(8,128)} %get-tuple-element.4) | data formatting | bytes 2359296
  143.9 0.0 copy-done
  143.9 1.0 copy.13
Async XLA Ops:
  141.5 2.5 %copy-start = (f32[768,384]{1,0:T(8,128)S(1)}, f32[768,384]{1,0:T(8,128)}, u32[]{:S(2)}) copy-start(f32[768,384]{1,0:T(8,128)} %get-tuple-element.5) | copy-start | bytes 3538948

commit v4 on v3

--- a/solution.py
+++ b/solution.py
@@ -79,9 +79,9 @@
 
 
 def fused_kernel(
-    n_seq, n_ten, tok_h, cot_h, wq_h, wk_h, wv_h, wo_h, nv_h, no_h, gv, go,
-    tok, cot, w3, wo, loc, recv, tmp, gath, cols, cols_t, acc, nv, no, probs, sq_seq, sq_ten,
-    in_sem, w_sem, own_sem, a2a_s, a2a_r, hs_s, hs_r, tk_s, tk_r, fw_s, fw_r,
+    n_seq, n_ten, tok_h, cot_h, wk_h, wq_h, wv_h, wo_h, made_v, made_o, factor_out,
+    tok, cot, w3, wo, loc, recv, tmp, gath, cols, cols_t, acc_v, acc_o, probs, sq_seq, sq_ten,
+    in_sem, w_sem, own_sem, out_sem, a2a_s, a2a_r, hs_s, hs_r, tk_s, tk_r, fw_s, fw_r,
     ag_s, ag_r, sib_s, sib_r, sq_s, sq_r, st_s, st_r,
 ):
     me = lax.axis_index("seq")
@@ -105,8 +105,6 @@
         pltpu.make_async_copy(wv_h, w3.at[2], w_sem.at[2]),
         pltpu.make_async_copy(cot_h, cot, in_sem.at[1]),
         pltpu.make_async_copy(wo_h, wo, w_sem.at[3]),
-        pltpu.make_async_copy(nv_h, nv, in_sem.at[2]),
-        pltpu.make_async_copy(no_h, no, in_sem.at[3]),
     ]
     for load in loads:
         load.start()
@@ -191,14 +189,14 @@
 
     held = (tok, cot)
 
+    def ten_rows(index):
+        return pl.ds(pl.multiple_of(index * quarter, quarter), quarter)
+
     def own_columns(which):
         return pltpu.make_async_copy(
-            held[which].at[:, pl.ds(pl.multiple_of(me * block, block), block)],
-            cols.at[which, me], own_sem.at[which],
-        )
-
-    def ten_rows(index):
-        return pl.ds(pl.multiple_of(index * quarter, quarter), quarter)
+            held[which].at[ten_rows(ten), pl.ds(pl.multiple_of(me * block, block), block)],
+            cols.at[which, me, ten_rows(ten), :], own_sem.at[which],
+        )
 
     def column_copy(which, step, source):
         peer = (me + step) % n_seq
@@ -211,15 +209,12 @@
             tk_s.at[which, step], tk_r.at[which, step], peer, ten,
         )
 
-    def column_share(which, step, hop, source):
-        origin = (me + n_seq - step) % n_seq
+    def column_share(which, hop, source):
         peer = (ten + hop) % n_ten
         if source:
             peer = (ten + n_ten - hop) % n_ten
-        piece = cols.at[which, origin, ten_rows(peer if source else ten), :]
-        return remote(
-            piece, piece, fw_s.at[which, step, hop], fw_r.at[which, step, hop], me, peer
-        )
+        piece = cols.at[which, :, ten_rows(peer if source else ten), :]
+        return remote(piece, piece, fw_s.at[which, hop], fw_r.at[which, hop], me, peer)
 
     def send_columns(which):
         own_columns(which).start()
@@ -233,26 +228,28 @@
         def _(step):
             column_copy(which, step, True).wait_recv()
 
-            @pl.loop(1, n_ten)
-            def _(hop):
-                column_share(which, step, hop, False).start()
-
         own_columns(which).wait()
+
+        @pl.loop(1, n_ten)
+        def _(hop):
+            column_share(which, hop, False).start()
 
     loads[0].wait()
     send_columns(0)
+    loads[4].wait()
+    send_columns(1)
     for kind in range(3):
         loads[1 + kind].wait()
         project(kind)
         send_heads(kind)
-    loads[4].wait()
     loads[5].wait()
     project(3)
     send_heads(3)
 
-    send_columns(1)
     pass_on(0)
+    share_columns(0)
     pass_on(1)
+    share_columns(1)
     have_heads(0)
     have_heads(1)
     blocks = patches // 256
@@ -348,15 +345,11 @@
             tmp[1, slot, strip(at), :] = d_value.T.astype(BF16)
 
     send_results(1)
-    share_columns(0)
-    share_columns(1)
 
     def turn_columns(which):
-        @pl.loop(1, n_seq)
-        def _(step):
-            @pl.loop(1, n_ten)
-            def _(hop):
-                column_share(which, step, hop, True).wait_recv()
+        @pl.loop(1, n_ten)
+        def _(hop):
+            column_share(which, hop, True).wait_recv()
 
         @pl.loop(0, n_seq)
         def _(origin):
@@ -381,17 +374,55 @@
         for part in range(2):
             sibling_copy(which, part, step, True).wait_recv()
 
+    def hand_out(which, image):
+        if which == 0:
+            return pltpu.make_async_copy(acc_o.at[image], made_o.at[image], out_sem.at[0, image])
+        return pltpu.make_async_copy(acc_v.at[image], made_v.at[image], out_sem.at[1, image])
+
     def multiply(which, image):
         @pl.loop(0, 3)
         def _(at):
             head = image * 6 + 2 * at
             heads = jnp.concatenate([gath[which, head], gath[which, head + 1]], axis=1)
             product = jnp.dot(cols_t[1 - which, image], heads, preferred_element_type=F32)
-            acc[which, image, at] = product
+            if which == 0:
+                acc_o[image, strip(at), :] = product.T
+            else:
+                acc_v[image, :, strip(at)] = product
             folded = jnp.sum((product * product).reshape(-1, 8, 256), axis=0)
             sq_seq[me, pl.ds(pl.multiple_of(image * 8, 8), 8), :] += (
                 folded[:, :HEAD_DIM] + folded[:, HEAD_DIM:]
             )
+
+        hand_out(which, image).start()
+
+    def finish_early():
+        for kind in range(4):
+            @pl.loop(1, n_chip)
+            def _(step):
+                exchange(kind, step, False).wait_send()
+
+            @pl.loop(0, n_chip)
+            def _(step):
+                pass_heads(kind, step, False).wait_send()
+
+        for which in range(2):
+            @pl.loop(1, n_seq)
+            def _(step):
+                column_copy(which, step, False).wait_send()
+
+            @pl.loop(1, n_ten)
+            def _(hop):
+                column_share(which, hop, False).wait_send()
+
+            for part in range(2):
+                @pl.loop(1, n_chip)
+                def _(step):
+                    plane_copy(which, part, step, False).wait_send()
+
+                @pl.loop(0, n_chip)
+                def _(step):
+                    sibling_copy(which, part, step, False).wait_send()
 
     sq_seq[me] = jnp.zeros((16, HEAD_DIM), F32)
     pass_results(0, partner_step)
@@ -411,6 +442,7 @@
     multiply(1, near)
     pass_results(1, far_steps[0])
     pass_results(1, far_steps[1])
+    finish_early()
     have_results(1, far_steps[0])
     have_results(1, far_steps[1])
     multiply(1, 1 - near)
@@ -436,48 +468,15 @@
     sq_ten[ten] = jnp.sum(sq_seq[...], axis=0)
     for step in range(1, n_ten):
         square_ten(step, False).start()
-    loads[6].wait()
-    loads[7].wait()
     for step in range(1, n_ten):
         square_ten(step, True).wait_recv()
     total = jnp.sum(sq_ten[...], axis=0)
     norm = jnp.sum(jnp.sum(total.reshape(2, 8, HEAD_DIM), axis=1), axis=1, keepdims=True)
     factor = math.sqrt(2.0 * width * width) / (jnp.sqrt(norm) + 0.01)
-    first, second = factor[0:1, :], factor[1:2, :]
-
-    @pl.loop(0, 3)
-    def _(at):
-        lanes = strip(at)
-        value = nv[:, lanes] + first * acc[1, 0, at] + second * acc[1, 1, at]
-        gv[:, lanes] = value * 0.5
-        mixed = first * acc[0, 0, at] + second * acc[0, 1, at]
-        go[lanes, :] = (no[lanes, :] + mixed.T) * 0.5
-
-    for kind in range(4):
-        @pl.loop(1, n_chip)
-        def _(step):
-            exchange(kind, step, False).wait_send()
-
-        @pl.loop(0, n_chip)
-        def _(step):
-            pass_heads(kind, step, False).wait_send()
+    factor_out[...] = jnp.broadcast_to(factor, (2, HEAD_DIM))
     for which in range(2):
-        @pl.loop(1, n_seq)
-        def _(step):
-            column_copy(which, step, False).wait_send()
-
-            @pl.loop(1, n_ten)
-            def _(hop):
-                column_share(which, step, hop, False).wait_send()
-
-        for part in range(2):
-            @pl.loop(1, n_chip)
-            def _(step):
-                plane_copy(which, part, step, False).wait_send()
-
-            @pl.loop(0, n_chip)
-            def _(step):
-                sibling_copy(which, part, step, False).wait_send()
+        for image in range(2):
+            hand_out(which, image).wait()
     for step in range(1, n_seq):
         square_seq(step, False).wait_send()
     for step in range(1, n_ten):
@@ -492,14 +491,19 @@
     rows, patches, block = images * patch, patch * n_seq, width // n_seq
     n_chip = n_seq // 2
     dma = pltpu.SemaphoreType.DMA
-    return pl.pallas_call(
+    made_v, made_o, factor = pl.pallas_call(
         functools.partial(fused_kernel, n_seq, n_ten),
         out_shape=(
-            jax.ShapeDtypeStruct(noise_value.shape, F32),
-            jax.ShapeDtypeStruct(noise_out.shape, F32),
+            jax.ShapeDtypeStruct((images, block, columns), F32),
+            jax.ShapeDtypeStruct((images, columns, block), F32),
+            jax.ShapeDtypeStruct((images, HEAD_DIM), F32),
         ),
-        in_specs=[pl.BlockSpec(memory_space=pl.ANY)] * 8,
-        out_specs=[pl.BlockSpec(memory_space=pltpu.VMEM)] * 2,
+        in_specs=[pl.BlockSpec(memory_space=pl.ANY)] * 6,
+        out_specs=[
+            pl.BlockSpec(memory_space=pl.ANY),
+            pl.BlockSpec(memory_space=pl.ANY),
+            pl.BlockSpec(memory_space=pltpu.VMEM),
+        ],
         scratch_shapes=[
             pltpu.VMEM((rows, width), BF16),
             pltpu.VMEM((rows, width), BF16),
@@ -511,23 +515,23 @@
             pltpu.VMEM((2, 12, patches, HEAD_DIM), BF16),
             pltpu.VMEM((2, n_seq, rows, block), BF16),
             pltpu.VMEM((2, 2, block, patches), BF16),
-            pltpu.VMEM((2, 2, 3, block, 256), F32),
-            pltpu.VMEM(noise_value.shape, F32),
-            pltpu.VMEM(noise_out.shape, F32),
+            pltpu.VMEM((images, block, columns), F32),
+            pltpu.VMEM((images, columns, block), F32),
             pltpu.VMEM((2, patches, patches), BF16),
             pltpu.VMEM((n_seq, 16, HEAD_DIM), F32),
             pltpu.VMEM((n_ten, 16, HEAD_DIM), F32),
-            dma((4,)),
+            dma((2,)),
             dma((4,)),
             dma((2,)),
+            dma((2, 2)),
             dma((4, n_chip)),
             dma((4, n_chip)),
             dma((4, n_chip)),
             dma((4, n_chip)),
             dma((2, n_seq)),
             dma((2, n_seq)),
-            dma((2, n_seq, n_ten)),
-            dma((2, n_seq, n_ten)),
+            dma((2, n_ten)),
+            dma((2, n_ten)),
             dma((2, 2, n_chip)),
             dma((2, 2, n_chip)),
             dma((2, 2, n_chip)),
@@ -542,7 +546,12 @@
         ),
     )(
         tokens.reshape(rows, width), cotangent.reshape(rows, width),
-        w_query, w_key, w_value, w_out, noise_value, noise_out,
+        w_key, w_query, w_value, w_out,
+    )
+    first, second = factor[0, 0], factor[1, 0]
+    return (
+        (noise_value + first * made_v[0] + second * made_v[1]) * 0.5,
+        (noise_out + first * made_o[0] + second * made_o[1]) * 0.5,
     )
 
 

time: 145 us -> 151 us (1.041)
  other arithmetic: 0 us -> 7.02 us
  local copies, waits for them, and re-layouts: 3.47 us -> 1.3 us
    mul x0 -> x2, other arithmetic: none -> 7.02 us  [the longest x1 4.53 us: local_fused(): (noise_out + first * made_o[0] + second * made_o[1]) * 0.5]
    unnamed x4 -> x6, local copies, waits for them, and re-layouts: 3.47 us -> 0.01 us
where the time goes in v4:
time: 151 us
  Pallas kernels  142 us (94%)
  other arithmetic  7.02 us (5%)
    pallas_call x1, Pallas kernels, local_fused(): pl.pallas_call(functools.partial(fused_kernel, n_seq, n_ten), out_shape=(...  142 us
    mul x1, other arithmetic, local_fused(): (noise_out + first * made_o[0] + second * made_o[1]) * 0.5  4.53 us

profile of v4, /device:TPU:0, one launch (start us, length us, event | category | flops | bytes accessed | tf_op | source)
XLA Modules:
  0.0 151.2 jit_solution(3636092244123734503)
XLA Ops:
  0.6 0.0 copy-start.1
  0.6 142.2 %shard_map.95 = (f32[2,384,768]{2,1,0:T(8,128)}, f32[2,768,384]{2,1,0:T(8,128)}, f32[2,128]{1,0:T(2,128)}) custom-call(bf16[256,3072]{1,0:T(8,128)(2,1)} %bitcast.20, bf16[256,3072]{1,0:T(8,128)(2,1)} %bitcast.21, bf16[3072,768]{1,0:T(8,128)(2,1)} %wk_h.1, bf16[3072,768]{1,0:T(8,128)(2,1)} %wq_h.1, bf16[3072,768]{1,0:T(8,128)(2,1)} %wv_h.1, ...), custom_call_target="tpu_custom_call" | custom-call | tf_op jit(solution)/shard_map/pallas_call | solution.py:494
  142.8 1.3 fusion.2
  144.1 0.0 copy-done.1
  144.1 0.0 copy-start
  144.1 0.0 copy-start.2
  144.1 4.5 %fusion = f32[768,384]{1,0:T(8,128)} fusion(f32[768,384]{1,0:T(8,128)S(1)} %copy-done.1, f32[2,768,384]{2,1,0:T(8,128)} %get-tuple-element.7, f32[]{:T(128)} %bitcast.4, f32[]{:T(128)} %bitcast.2), kind=kLoop, calls=%fused_computation.1 | loop fusion | flops 1474560 | bytes 4718600 | tf_op jit(solution)/shard_map/mul | solution.py:554
  148.7 0.0 copy-done
  148.7 0.0 copy-done.2
  148.7 2.5 %fusion.1 = f32[384,768]{1,0:T(8,128)} fusion(f32[384,768]{1,0:T(8,128)S(1)} %copy-done.2, f32[2,384,768]{2,1,0:T(8,128)S(1)} %copy-done, f32[]{:T(128)} %bitcast.4, f32[]{:T(128)} %bitcast.2), kind=kLoop, calls=%fused_computation.4 | loop fusion | flops 1474560 | bytes 4718600 | tf_op jit(solution)/shard_map/mul | solution.py:553
Async XLA Ops:
  0.6 143.5 %copy-start.1 = (f32[768,384]{1,0:T(8,128)S(1)}, f32[768,384]{1,0:T(8,128)}, u32[]{:S(2)}) copy-start(f32[768,384]{1,0:T(8,128)} %param.15) | copy-start | bytes 3538948
  144.1 4.5 %copy-start = (f32[2,384,768]{2,1,0:T(8,128)S(1)}, f32[2,384,768]{2,1,0:T(8,128)}, u32[]{:S(2)}) copy-start(f32[2,384,768]{2,1,0:T(8,128)} %get-tuple-element.6) | copy-start | bytes 7077892
  144.1 4.5 %copy-start.2 = (f32[384,768]{1,0:T(8,128)S(1)}, f32[384,768]{1,0:T(8,128)}, u32[]{:S(2)}) copy-start(f32[384,768]{1,0:T(8,128)} %param.14) | copy-start | bytes 3538948

commit v5 on v4

--- a/solution.py
+++ b/solution.py
@@ -79,9 +79,9 @@
 
 
 def fused_kernel(
-    n_seq, n_ten, tok_h, cot_h, wk_h, wq_h, wv_h, wo_h, made_v, made_o, factor_out,
-    tok, cot, w3, wo, loc, recv, tmp, gath, cols, cols_t, acc_v, acc_o, probs, sq_seq, sq_ten,
-    in_sem, w_sem, own_sem, out_sem, a2a_s, a2a_r, hs_s, hs_r, tk_s, tk_r, fw_s, fw_r,
+    n_seq, n_ten, tok_h, cot_h, wk_h, wq_h, wv_h, wo_h, nv_h, no_h, gv, go,
+    tok, cot, w3, wo, loc, recv, tmp, gath, cols, cols_t, acc_v, acc_o, nv, no, probs, sq_seq, sq_ten,
+    in_sem, w_sem, own_sem, a2a_s, a2a_r, hs_s, hs_r, tk_s, tk_r, fw_s, fw_r,
     ag_s, ag_r, sib_s, sib_r, sq_s, sq_r, st_s, st_r,
 ):
     me = lax.axis_index("seq")
@@ -105,6 +105,8 @@
         pltpu.make_async_copy(wv_h, w3.at[2], w_sem.at[2]),
         pltpu.make_async_copy(cot_h, cot, in_sem.at[1]),
         pltpu.make_async_copy(wo_h, wo, w_sem.at[3]),
+        pltpu.make_async_copy(nv_h, nv, in_sem.at[2]),
+        pltpu.make_async_copy(no_h, no, in_sem.at[3]),
     ]
     for load in loads:
         load.start()
@@ -236,20 +238,19 @@
 
     loads[0].wait()
     send_columns(0)
-    loads[4].wait()
-    send_columns(1)
     for kind in range(3):
         loads[1 + kind].wait()
         project(kind)
         send_heads(kind)
+    loads[4].wait()
     loads[5].wait()
     project(3)
     send_heads(3)
+    send_columns(1)
 
     pass_on(0)
     share_columns(0)
     pass_on(1)
-    share_columns(1)
     have_heads(0)
     have_heads(1)
     blocks = patches // 256
@@ -284,39 +285,36 @@
             return gath.at[which, own_head(at_chip, at_core)]
         return gath.at[which, shared_head(at_chip), half_rows(at_core), :]
 
-    def made(which, part):
-        if part == 0:
-            return tmp.at[which, core]
-        return tmp.at[which, 1 - core, half_rows(core), :]
-
-    def plane_copy(which, part, step, source):
-        other = (chip + step) % n_chip
-        if source:
-            other = (chip + n_chip - step) % n_chip
+    near = chip // 2
+    partner = 4 * near + 1 - chip
+    far_mid = 2 - near
+    far_outer = 3 - 3 * near
+    in_middle = (chip + near) % 2 == 1
+
+    def block_copy(which, part, origin, to, slot):
+        piece = place(which, part, origin, core)
         return remote(
-            made(which, part), place(which, part, other if source else chip, core),
-            ag_s.at[which, part, step], ag_r.at[which, part, step], 2 * other + core, ten,
-        )
-
-    def sibling_copy(which, part, step, source):
-        origin = (chip + n_chip - step) % n_chip
+            piece, piece, ag_s.at[which, part, slot], ag_r.at[which, part, origin],
+            2 * to + core, ten,
+        )
+
+    def sibling_copy(which, part, origin, source):
         piece = place(which, part, origin, 1 - core if source else core)
         return remote(
-            piece, piece, sib_s.at[which, part, step], sib_r.at[which, part, step], sibling, ten
+            piece, piece, sib_s.at[which, part, origin], sib_r.at[which, part, origin],
+            sibling, ten,
         )
 
     def send_results(which):
-        for part in range(2):
-            @pl.loop(1, n_chip)
-            def _(step):
-                plane_copy(which, part, step, False).start()
-
         gath[which, own_head(chip, core)] = tmp[which, core]
         gath[which, shared_head(chip), half_rows(core), :] = tmp[
             which, 1 - core, half_rows(core), :
         ]
         for part in range(2):
-            sibling_copy(which, part, 0, False).start()
+            block_copy(which, part, chip, far_mid, 1).start()
+            block_copy(which, part, chip, partner, 0).start()
+        for part in range(2):
+            sibling_copy(which, part, chip, False).start()
 
     pass_on(2)
     have_heads(2)
@@ -345,6 +343,7 @@
             tmp[1, slot, strip(at), :] = d_value.T.astype(BF16)
 
     send_results(1)
+    share_columns(1)
 
     def turn_columns(which):
         @pl.loop(1, n_ten)
@@ -358,26 +357,18 @@
                 piece = cols[which, origin, image * patch:(image + 1) * patch, :]
                 cols_t[which, image, :, lanes] = piece.T
 
-    near = chip // 2
-    partner = chip + 1 - 2 * (chip % 2)
-    partner_step = (chip + n_chip - partner) % n_chip
-    far_steps = [
-        (chip + n_chip - (2 * (1 - near) + at)) % n_chip for at in range(2)
-    ]
-
-    def pass_results(which, step):
+    def pass_results(which, origin, slot):
         for part in range(2):
-            plane_copy(which, part, step, True).wait_recv()
-            sibling_copy(which, part, step, False).start()
-
-    def have_results(which, step):
+            block_copy(which, part, origin, partner, slot).wait_recv()
+            if slot > 0:
+                @pl.when(in_middle)
+                def _():
+                    block_copy(which, part, origin, partner, slot).start()
+            sibling_copy(which, part, origin, False).start()
+
+    def have_results(which, origin):
         for part in range(2):
-            sibling_copy(which, part, step, True).wait_recv()
-
-    def hand_out(which, image):
-        if which == 0:
-            return pltpu.make_async_copy(acc_o.at[image], made_o.at[image], out_sem.at[0, image])
-        return pltpu.make_async_copy(acc_v.at[image], made_v.at[image], out_sem.at[1, image])
+            sibling_copy(which, part, origin, True).wait_recv()
 
     def multiply(which, image):
         @pl.loop(0, 3)
@@ -394,8 +385,6 @@
                 folded[:, :HEAD_DIM] + folded[:, HEAD_DIM:]
             )
 
-        hand_out(which, image).start()
-
     def finish_early():
         for kind in range(4):
             @pl.loop(1, n_chip)
@@ -416,35 +405,39 @@
                 column_share(which, hop, False).wait_send()
 
             for part in range(2):
-                @pl.loop(1, n_chip)
-                def _(step):
-                    plane_copy(which, part, step, False).wait_send()
+                block_copy(which, part, chip, partner, 0).wait_send()
+                block_copy(which, part, chip, far_mid, 1).wait_send()
+
+                @pl.when(in_middle)
+                def _():
+                    block_copy(which, part, far_mid, partner, 2).wait_send()
+                    block_copy(which, part, far_outer, partner, 3).wait_send()
 
                 @pl.loop(0, n_chip)
-                def _(step):
-                    sibling_copy(which, part, step, False).wait_send()
+                def _(origin):
+                    sibling_copy(which, part, origin, False).wait_send()
 
     sq_seq[me] = jnp.zeros((16, HEAD_DIM), F32)
-    pass_results(0, partner_step)
+    pass_results(0, partner, 0)
+    pass_results(0, far_mid, 2)
+    pass_results(0, far_outer, 3)
+    turn_columns(0)
+    pass_results(1, partner, 0)
     turn_columns(1)
-    pass_results(0, far_steps[0])
-    pass_results(0, far_steps[1])
-    pass_results(1, partner_step)
-    turn_columns(0)
-    have_results(0, 0)
-    have_results(0, partner_step)
+    have_results(0, chip)
+    have_results(0, partner)
     multiply(0, near)
-    have_results(0, far_steps[0])
-    have_results(0, far_steps[1])
+    pass_results(1, far_mid, 2)
+    have_results(0, far_mid)
+    have_results(0, far_outer)
     multiply(0, 1 - near)
-    have_results(1, 0)
-    have_results(1, partner_step)
+    pass_results(1, far_outer, 3)
+    have_results(1, chip)
+    have_results(1, partner)
     multiply(1, near)
-    pass_results(1, far_steps[0])
-    pass_results(1, far_steps[1])
     finish_early()
-    have_results(1, far_steps[0])
-    have_results(1, far_steps[1])
+    have_results(1, far_mid)
+    have_results(1, far_outer)
     multiply(1, 1 - near)
 
     def square_seq(step, source):
@@ -473,10 +466,18 @@
     total = jnp.sum(sq_ten[...], axis=0)
     norm = jnp.sum(jnp.sum(total.reshape(2, 8, HEAD_DIM), axis=1), axis=1, keepdims=True)
     factor = math.sqrt(2.0 * width * width) / (jnp.sqrt(norm) + 0.01)
-    factor_out[...] = jnp.broadcast_to(factor, (2, HEAD_DIM))
-    for which in range(2):
-        for image in range(2):
-            hand_out(which, image).wait()
+    first, second = factor[0:1, :], factor[1:2, :]
+    loads[6].wait()
+    loads[7].wait()
+
+    @pl.loop(0, 3)
+    def _(at):
+        lanes = strip(at)
+        value = nv[:, lanes] + first * acc_v[0, :, lanes] + second * acc_v[1, :, lanes]
+        gv[:, lanes] = value * 0.5
+        value = no[lanes, :] + first * acc_o[0, lanes, :] + second * acc_o[1, lanes, :]
+        go[lanes, :] = value * 0.5
+
     for step in range(1, n_seq):
         square_seq(step, False).wait_send()
     for step in range(1, n_ten):
@@ -491,19 +492,14 @@
     rows, patches, block = images * patch, patch * n_seq, width // n_seq
     n_chip = n_seq // 2
     dma = pltpu.SemaphoreType.DMA
-    made_v, made_o, factor = pl.pallas_call(
+    return pl.pallas_call(
         functools.partial(fused_kernel, n_seq, n_ten),
         out_shape=(
-            jax.ShapeDtypeStruct((images, block, columns), F32),
-            jax.ShapeDtypeStruct((images, columns, block), F32),
-            jax.ShapeDtypeStruct((images, HEAD_DIM), F32),
+            jax.ShapeDtypeStruct(noise_value.shape, F32),
+            jax.ShapeDtypeStruct(noise_out.shape, F32),
         ),
-        in_specs=[pl.BlockSpec(memory_space=pl.ANY)] * 6,
-        out_specs=[
-            pl.BlockSpec(memory_space=pl.ANY),
-            pl.BlockSpec(memory_space=pl.ANY),
-            pl.BlockSpec(memory_space=pltpu.VMEM),
-        ],
+        in_specs=[pl.BlockSpec(memory_space=pl.ANY)] * 8,
+        out_specs=[pl.BlockSpec(memory_space=pltpu.VMEM)] * 2,
         scratch_shapes=[
             pltpu.VMEM((rows, width), BF16),
             pltpu.VMEM((rows, width), BF16),
@@ -517,13 +513,14 @@
             pltpu.VMEM((2, 2, block, patches), BF16),
             pltpu.VMEM((images, block, columns), F32),
             pltpu.VMEM((images, columns, block), F32),
+            pltpu.VMEM(noise_value.shape, F32),
+            pltpu.VMEM(noise_out.shape, F32),
             pltpu.VMEM((2, patches, patches), BF16),
             pltpu.VMEM((n_seq, 16, HEAD_DIM), F32),
             pltpu.VMEM((n_ten, 16, HEAD_DIM), F32),
-            dma((2,)),
+            dma((4,)),
             dma((4,)),
             dma((2,)),
-            dma((2, 2)),
             dma((4, n_chip)),
             dma((4, n_chip)),
             dma((4, n_chip)),
@@ -546,12 +543,7 @@
         ),
     )(
         tokens.reshape(rows, width), cotangent.reshape(rows, width),
-        w_key, w_query, w_value, w_out,
-    )
-    first, second = factor[0, 0], factor[1, 0]
-    return (
-        (noise_value + first * made_v[0] + second * made_v[1]) * 0.5,
-        (noise_out + first * made_o[0] + second * made_o[1]) * 0.5,
+        w_key, w_query, w_value, w_out, noise_value, noise_out,
     )
 
 

time: 151 us -> 131 us (0.87)
  Pallas kernels: 142 us -> 127 us
  other arithmetic: 7.02 us -> 0 us
  local copies, waits for them, and re-layouts: 1.3 us -> 3.47 us
    pallas_call x1, Pallas kernels: 142 us -> 127 us  [local_fused(): pl.pallas_call(functools.partial(fused_kernel, n_seq, n_ten), out_shape=(...]
    mul x2 -> x0, other arithmetic: 7.02 us -> none  [the longest x1 4.53 us: local_fused(): (noise_out + first * made_o[0] + second * made_o[1]) * 0.5]
    unnamed x6 -> x4, local copies, waits for them, and re-layouts: 0.01 us -> 3.47 us
where the time goes in v5:
time: 131 us
  Pallas kernels  127 us (97%)
  local copies, waits for them, and re-layouts  3.47 us (3%)
    pallas_call x1, Pallas kernels, local_fused(): pl.pallas_call(functools.partial(fused_kernel, n_seq, n_ten), out_shape=(...  127 us
    unnamed x4, local copies, waits for them, and re-layouts  3.47 us

profile of v5, /device:TPU:0, one launch (start us, length us, event | category | flops | bytes accessed | tf_op | source)
XLA Modules:
  0.0 130.9 jit_solution(11002270832572707814)
XLA Ops:
  0.6 126.8 %shard_map.95 = (f32[384,768]{1,0:T(8,128)}, f32[768,384]{1,0:T(8,128)}) custom-call(bf16[256,3072]{1,0:T(8,128)(2,1)} %bitcast.2, bf16[256,3072]{1,0:T(8,128)(2,1)} %bitcast.3, bf16[3072,768]{1,0:T(8,128)(2,1)} %wk_h.1, bf16[3072,768]{1,0:T(8,128)(2,1)} %wq_h.1, bf16[3072,768]{1,0:T(8,128)(2,1)} %wv_h.1, bf16[768,3072]{1,0:T(8,128)(2,1)} %wo_h.1, ...), custom_call_target="tpu_custom_call" | custom-call | tf_op jit(solution)/shard_map/pallas_call | solution.py:495
  127.4 0.0 copy-start
  127.5 2.5 %copy.12 = f32[384,768]{1,0:T(8,128)} copy(f32[384,768]{1,0:T(8,128)} %get-tuple-element.4) | data formatting | bytes 2359296
  129.9 0.0 copy-done
  129.9 1.0 copy.13
Async XLA Ops:
  127.4 2.5 %copy-start = (f32[768,384]{1,0:T(8,128)S(1)}, f32[768,384]{1,0:T(8,128)}, u32[]{:S(2)}) copy-start(f32[768,384]{1,0:T(8,128)} %get-tuple-element.5) | copy-start | bytes 3538948

commit v6 on v5

--- a/solution.py
+++ b/solution.py
@@ -258,8 +258,7 @@
     def strip(at):
         return pl.ds(pl.multiple_of(at * 256, 256), 256)
 
-    @pl.loop(0, 2)
-    def _(slot):
+    def score(slot):
         @pl.loop(0, blocks)
         def _(at):
             scores = lax.dot_general(
@@ -271,56 +270,7 @@
             total = jnp.sum(raised, axis=1, keepdims=True)
             probs[slot, strip(at), :] = (raised * (1.0 / total)).astype(BF16)
 
-    def own_head(at_chip, at_core):
-        return (at_chip // 2) * 6 + 3 * (at_chip % 2) + 2 * at_core
-
-    def shared_head(at_chip):
-        return (at_chip // 2) * 6 + 3 * (at_chip % 2) + 1
-
-    def half_rows(at_core):
-        return pl.ds(pl.multiple_of(at_core * half, half), half)
-
-    def place(which, part, at_chip, at_core):
-        if part == 0:
-            return gath.at[which, own_head(at_chip, at_core)]
-        return gath.at[which, shared_head(at_chip), half_rows(at_core), :]
-
-    near = chip // 2
-    partner = 4 * near + 1 - chip
-    far_mid = 2 - near
-    far_outer = 3 - 3 * near
-    in_middle = (chip + near) % 2 == 1
-
-    def block_copy(which, part, origin, to, slot):
-        piece = place(which, part, origin, core)
-        return remote(
-            piece, piece, ag_s.at[which, part, slot], ag_r.at[which, part, origin],
-            2 * to + core, ten,
-        )
-
-    def sibling_copy(which, part, origin, source):
-        piece = place(which, part, origin, 1 - core if source else core)
-        return remote(
-            piece, piece, sib_s.at[which, part, origin], sib_r.at[which, part, origin],
-            sibling, ten,
-        )
-
-    def send_results(which):
-        gath[which, own_head(chip, core)] = tmp[which, core]
-        gath[which, shared_head(chip), half_rows(core), :] = tmp[
-            which, 1 - core, half_rows(core), :
-        ]
-        for part in range(2):
-            block_copy(which, part, chip, far_mid, 1).start()
-            block_copy(which, part, chip, partner, 0).start()
-        for part in range(2):
-            sibling_copy(which, part, chip, False).start()
-
-    pass_on(2)
-    have_heads(2)
-
-    @pl.loop(0, 2)
-    def _(slot):
+    def attend(slot):
         @pl.loop(0, blocks)
         def _(at):
             attended = jnp.dot(
@@ -328,21 +278,71 @@
             )
             tmp[0, slot, strip(at), :] = attended.astype(BF16)
 
-    send_results(0)
+    def pull_back(slot):
+        d_value = lax.dot_general(
+            recv[3, core + slot], probs[slot], DEPTH_DOT, preferred_element_type=F32
+        )
+        tmp[1, slot] = d_value.T.astype(BF16)
+
+    def own_head(at_chip, at_core):
+        return (at_chip // 2) * 6 + 3 * (at_chip % 2) + 2 * at_core
+
+    def shared_head(at_chip):
+        return (at_chip // 2) * 6 + 3 * (at_chip % 2) + 1
+
+    def half_rows(at_core):
+        return pl.ds(pl.multiple_of(at_core * half, half), half)
+
+    def place(which, part, at_chip, at_core):
+        if part == 0:
+            return gath.at[which, own_head(at_chip, at_core)]
+        return gath.at[which, shared_head(at_chip), half_rows(at_core), :]
+
+    near = chip // 2
+    partner = 4 * near + 1 - chip
+    far_mid = 2 - near
+    far_outer = 3 - 3 * near
+    in_middle = (chip + near) % 2 == 1
+
+    def block_copy(which, part, origin, to, slot):
+        piece = place(which, part, origin, core)
+        return remote(
+            piece, piece, ag_s.at[which, part, slot], ag_r.at[which, part, origin],
+            2 * to + core, ten,
+        )
+
+    def sibling_copy(which, part, origin, source):
+        piece = place(which, part, origin, 1 - core if source else core)
+        return remote(
+            piece, piece, sib_s.at[which, part, origin], sib_r.at[which, part, origin],
+            sibling, ten,
+        )
+
+    def send_part(which, part):
+        if part == 0:
+            gath[which, own_head(chip, core)] = tmp[which, core]
+        else:
+            gath[which, shared_head(chip), half_rows(core), :] = tmp[
+                which, 1 - core, half_rows(core), :
+            ]
+        block_copy(which, part, chip, far_mid, 1).start()
+        block_copy(which, part, chip, partner, 0).start()
+        sibling_copy(which, part, chip, False).start()
+
+    score(core)
+    pass_on(2)
+    have_heads(2)
+    attend(core)
+    send_part(0, 0)
+    score(1 - core)
+    attend(1 - core)
+    send_part(0, 1)
     pass_on(3)
     have_heads(3)
-
-    @pl.loop(0, 2)
-    def _(slot):
-        @pl.loop(0, blocks)
-        def _(at):
-            d_value = lax.dot_general(
-                recv[3, core + slot], probs[slot, :, strip(at)], DEPTH_DOT,
-                preferred_element_type=F32,
-            )
-            tmp[1, slot, strip(at), :] = d_value.T.astype(BF16)
-
-    send_results(1)
+    pull_back(core)
+    send_part(1, 0)
+    pull_back(1 - core)
+    send_part(1, 1)
     share_columns(1)
 
     def turn_columns(which):

time: 131 us -> 131 us (level)
  no operation moved by 1% of the time
where the time goes in v6:
time: 131 us
  Pallas kernels  127 us (97%)
  local copies, waits for them, and re-layouts  3.47 us (3%)
    pallas_call x1, Pallas kernels, local_fused(): pl.pallas_call(functools.partial(fused_kernel, n_seq, n_ten), out_shape=(...  127 us
    unnamed x4, local copies, waits for them, and re-layouts  3.47 us

profile of v6, /device:TPU:0, one launch (start us, length us, event | category | flops | bytes accessed | tf_op | source)
XLA Modules:
  0.0 130.7 jit_solution(8414069667980161450)
XLA Ops:
  0.6 126.6 %shard_map.95 = (f32[384,768]{1,0:T(8,128)}, f32[768,384]{1,0:T(8,128)}) custom-call(bf16[256,3072]{1,0:T(8,128)(2,1)} %bitcast.2, bf16[256,3072]{1,0:T(8,128)(2,1)} %bitcast.3, bf16[3072,768]{1,0:T(8,128)(2,1)} %wk_h.1, bf16[3072,768]{1,0:T(8,128)(2,1)} %wq_h.1, bf16[3072,768]{1,0:T(8,128)(2,1)} %wv_h.1, bf16[768,3072]{1,0:T(8,128)(2,1)} %wo_h.1, ...), custom_call_target="tpu_custom_call" | custom-call | tf_op jit(solution)/shard_map/pallas_call | solution.py:495
  127.2 0.0 copy-start
  127.2 2.5 %copy.12 = f32[384,768]{1,0:T(8,128)} copy(f32[384,768]{1,0:T(8,128)} %get-tuple-element.4) | data formatting | bytes 2359296
  129.7 0.0 copy-done
  129.7 1.0 copy.13
Async XLA Ops:
  127.2 2.5 %copy-start = (f32[768,384]{1,0:T(8,128)S(1)}, f32[768,384]{1,0:T(8,128)}, u32[]{:S(2)}) copy-start(f32[768,384]{1,0:T(8,128)} %get-tuple-element.5) | copy-start | bytes 3538948

commit v7 on v6

--- a/solution.py
+++ b/solution.py
@@ -357,13 +357,11 @@
                 piece = cols[which, origin, image * patch:(image + 1) * patch, :]
                 cols_t[which, image, :, lanes] = piece.T
 
-    def pass_results(which, origin, slot):
+    def pass_results(which, origin, slot, forward):
         for part in range(2):
             block_copy(which, part, origin, partner, slot).wait_recv()
-            if slot > 0:
-                @pl.when(in_middle)
-                def _():
-                    block_copy(which, part, origin, partner, slot).start()
+            if forward:
+                block_copy(which, part, origin, partner, slot).start()
             sibling_copy(which, part, origin, False).start()
 
     def have_results(which, origin):
@@ -418,20 +416,42 @@
                     sibling_copy(which, part, origin, False).wait_send()
 
     sq_seq[me] = jnp.zeros((16, HEAD_DIM), F32)
-    pass_results(0, partner, 0)
-    pass_results(0, far_mid, 2)
-    pass_results(0, far_outer, 3)
-    turn_columns(0)
-    pass_results(1, partner, 0)
-    turn_columns(1)
-    have_results(0, chip)
-    have_results(0, partner)
-    multiply(0, near)
-    pass_results(1, far_mid, 2)
-    have_results(0, far_mid)
-    have_results(0, far_outer)
-    multiply(0, 1 - near)
-    pass_results(1, far_outer, 3)
+    def multiply_early():
+        have_results(0, chip)
+        have_results(0, partner)
+        multiply(0, near)
+
+    def multiply_late():
+        have_results(0, far_mid)
+        have_results(0, far_outer)
+        multiply(0, 1 - near)
+
+    @pl.when(in_middle)
+    def _():
+        pass_results(0, partner, 0, False)
+        pass_results(0, far_mid, 2, True)
+        pass_results(0, far_outer, 3, True)
+        turn_columns(0)
+        pass_results(1, partner, 0, False)
+        pass_results(1, far_mid, 2, True)
+        pass_results(1, far_outer, 3, True)
+        turn_columns(1)
+        multiply_early()
+        multiply_late()
+
+    @pl.when(jnp.logical_not(in_middle))
+    def _():
+        pass_results(0, partner, 0, False)
+        turn_columns(0)
+        pass_results(1, partner, 0, False)
+        turn_columns(1)
+        multiply_early()
+        pass_results(0, far_mid, 2, False)
+        pass_results(0, far_outer, 3, False)
+        pass_results(1, far_mid, 2, False)
+        multiply_late()
+        pass_results(1, far_outer, 3, False)
+
     have_results(1, chip)
     have_results(1, partner)
     multiply(1, near)

time: 131 us -> 131 us (level)
  no operation moved by 1% of the time
where the time goes in v7:
time: 131 us
  Pallas kernels  127 us (97%)
  local copies, waits for them, and re-layouts  3.47 us (3%)
    pallas_call x1, Pallas kernels, local_fused(): pl.pallas_call(functools.partial(fused_kernel, n_seq, n_ten), out_shape=(...  127 us
    unnamed x4, local copies, waits for them, and re-layouts  3.47 us

profile of v7, /device:TPU:0, one launch (start us, length us, event | category | flops | bytes accessed | tf_op | source)
XLA Modules:
  0.0 130.7 jit_solution(12561966646959842069)
XLA Ops:
  0.6 126.6 %shard_map.95 = (f32[384,768]{1,0:T(8,128)}, f32[768,384]{1,0:T(8,128)}) custom-call(bf16[256,3072]{1,0:T(8,128)(2,1)} %bitcast.2, bf16[256,3072]{1,0:T(8,128)(2,1)} %bitcast.3, bf16[3072,768]{1,0:T(8,128)(2,1)} %wk_h.1, bf16[3072,768]{1,0:T(8,128)(2,1)} %wq_h.1, bf16[3072,768]{1,0:T(8,128)(2,1)} %wv_h.1, bf16[768,3072]{1,0:T(8,128)(2,1)} %wo_h.1, ...), custom_call_target="tpu_custom_call" | custom-call | tf_op jit(solution)/shard_map/pallas_call | solution.py:515
  127.2 0.0 copy-start
  127.3 2.5 %copy.12 = f32[384,768]{1,0:T(8,128)} copy(f32[384,768]{1,0:T(8,128)} %get-tuple-element.4) | data formatting | bytes 2359296
  129.7 0.0 copy-done
  129.7 1.0 copy.13
Async XLA Ops:
  127.2 2.5 %copy-start = (f32[768,384]{1,0:T(8,128)S(1)}, f32[768,384]{1,0:T(8,128)}, u32[]{:S(2)}) copy-start(f32[768,384]{1,0:T(8,128)} %get-tuple-element.5) | copy-start | bytes 3538948
